TPU v7x, 256 devices: a whole 4x4x8 slice. The times are simulated.
256 devices in a mesh: grp: 32 (over y, z), seq: 8 (over x, core).
Axes of the slice: x: 4, y: 4, z: 8, core: 2. Of those that a mesh axis runs over, the one named last changes fastest.
Arguments:
- queries: bfloat16 [65536, 1280], P(('grp', 'seq')), may hold values from -24 to 24
- key_rows: bfloat16 [65536, 1280], P(('grp', 'seq')), may hold values from -24 to 24
- values: bfloat16 [65536, 1280], P(('grp', 'seq')), may hold values from -6 to 6
- segment_ids: int32 [65536], P(('grp', 'seq')), may hold values from 0 to 511, as said below
- merger_norm_gain: float32 [1280], replicated, may hold values from 0.5 to 1.5
- merge_weight: bfloat16 [5120, 8192], P('grp', 'seq'), may hold values from -0.078125 to 0.078125
- text_rows: bfloat16 [32768, 8192], P(('grp', 'seq')), may hold values from -6 to 6
- token_gain: float32 [8192], replicated, may hold values from 0.5 to 1.5
- cotangent: bfloat16 [32768, 8192], P(('grp', 'seq')), may hold values from -6 to 6
- send_slot: int32 [16384], P(('grp', 'seq')), may hold values from 0 to 63, as said below
- place_pos: int32 [16384], P(('grp', 'seq')), may hold values from 0 to 127, as said below
Outputs:
- hidden: bfloat16 [32768, 8192], P(('grp', 'seq'))
- vision_output_gradient: bfloat16 [65536, 1280], P(('grp', 'seq'))
Inputs may be any that keep to these rules, and one draw needn't show every extreme that they name: `segment_ids`: ids are never smaller than the previous patch's within a group of 2048 patches; patches of one image share an id and come in runs whose length is a multiple of 4; image sizes differ from group to group. `send_slot`: within each device's 64 rows a permutation of 0 to 63; slot c goes to language replica c // 2. `place_pos`: within each device's 64 entries all positions differ.
All inputs are finite; a program needn't handle non-finite values.
Results may differ from a plain program's by a relative error of at most 0.019.
Values may be sent and summed in bfloat16 or wider, within the bound.
A program may use at most 128 MiB of HBM per device.

v0:
```python
import math

import jax
import jax.numpy as jnp
from jax import lax
from jax.sharding import PartitionSpec as P

VISION_WIDTH = 1280
HEAD_DIM = 80
MERGER_FEATURES = 5120
DEVICE_VIS_ROWS = 64


EPS = 1e-06


def head_attention(q_all, k_all, v_all, images):
    total = q_all.shape[0]
    local_heads = q_all.shape[1] // HEAD_DIM
    q_three = q_all.reshape(total, local_heads, HEAD_DIM)
    k_three = k_all.reshape(total, local_heads, HEAD_DIM)
    v_three = v_all.reshape(total, local_heads, HEAD_DIM)
    block_rows = math.gcd(512, total)
    score_scale = HEAD_DIM ** (-0.5)

    def one_block(index):
        lower = index * block_rows
        q_block = lax.dynamic_slice_in_dim(q_three, lower, block_rows, 0)
        own_images = lax.dynamic_slice_in_dim(images, lower, block_rows, 0)
        scores = (
            jnp.einsum("qhd,khd->hqk", q_block, k_three, preferred_element_type=jnp.float32)
            * score_scale
        )
        same_image = own_images[:, None] == images[None, :]
        scores = jnp.where(same_image[None], scores, -1e30)
        probs = jax.nn.softmax(scores, axis=-1).astype(jnp.bfloat16)
        output = jnp.einsum("hqk,khd->qhd", probs, v_three, preferred_element_type=jnp.float32)
        return output.astype(jnp.bfloat16).reshape(block_rows, local_heads * HEAD_DIM)

    blocks = lax.map(one_block, jnp.arange(total // block_rows, dtype=jnp.int32))
    return blocks.reshape(total, local_heads * HEAD_DIM)


def body(
    queries,
    key_rows,
    values,
    segment_ids,
    merger_norm_gain,
    merge_weight,
    text_rows,
    token_gain,
    cotangent,
    send_slot,
    place_pos,
):
    q_all, k_all, v_all = (
        lax.all_to_all(queries, "seq", split_axis=1, concat_axis=0, tiled=True),
        lax.all_to_all(key_rows, "seq", split_axis=1, concat_axis=0, tiled=True),
        lax.all_to_all(values, "seq", split_axis=1, concat_axis=0, tiled=True),
    )
    images = lax.all_gather(segment_ids, "seq", axis=0, tiled=True)
    attended = head_attention(q_all, k_all, v_all, images)
    attn = lax.all_to_all(attended, "seq", split_axis=0, concat_axis=1, tiled=True)
    patch_x = attn.astype(jnp.float32)
    mean_removed = patch_x - jnp.mean(patch_x, axis=-1, keepdims=True)
    inverse_deviation = lax.rsqrt(
        jnp.mean(mean_removed * mean_removed, axis=-1, keepdims=True) + EPS
    )
    normalized_rows = mean_removed * inverse_deviation
    merged_patches = (
        (normalized_rows * merger_norm_gain)
        .astype(jnp.bfloat16)
        .reshape(DEVICE_VIS_ROWS, MERGER_FEATURES)
    )
    w_columns = lax.all_gather(merge_weight, "grp", axis=0, tiled=True)
    projected = jnp.dot(
        lax.all_gather(merged_patches, "seq", axis=0, tiled=True),
        w_columns,
        preferred_element_type=jnp.float32,
    ).astype(jnp.bfloat16)
    own_rows = lax.all_to_all(projected, "seq", split_axis=0, concat_axis=1, tiled=True)
    slotted = jnp.zeros_like(own_rows).at[send_slot].set(own_rows)
    arrived = lax.all_to_all(slotted, "grp", split_axis=0, concat_axis=0, tiled=True)
    inputs = text_rows.at[place_pos].set(arrived).astype(jnp.float32)
    inv_rms = lax.rsqrt(jnp.mean(inputs * inputs, axis=-1, keepdims=True) + EPS)
    hidden = (inputs * inv_rms * token_gain).astype(jnp.bfloat16)
    grad_y = cotangent.astype(jnp.float32) * token_gain
    input_grads = inv_rms * (
        grad_y - inputs * inv_rms * inv_rms * jnp.mean(grad_y * inputs, axis=-1, keepdims=True)
    )
    back_rows = input_grads[place_pos].astype(jnp.bfloat16)
    slot_grads = lax.all_to_all(back_rows, "grp", split_axis=0, concat_axis=0, tiled=True)
    natural_grads = slot_grads[send_slot]
    returned = lax.all_to_all(natural_grads, "seq", split_axis=1, concat_axis=0, tiled=True)
    merged_gradient = lax.psum_scatter(
        lax.dot_general(
            returned, w_columns, (((1,), (1,)), ((), ())), preferred_element_type=jnp.float32
        ).astype(jnp.bfloat16),
        "seq",
        scatter_dimension=0,
        tiled=True,
    ).astype(jnp.float32)
    patch_gradient = (
        merged_gradient.reshape(normalized_rows.shape[0], VISION_WIDTH) * merger_norm_gain
    )
    vision_output_gradient = inverse_deviation * (
        patch_gradient
        - jnp.mean(patch_gradient, axis=-1, keepdims=True)
        - normalized_rows * jnp.mean(patch_gradient * normalized_rows, axis=-1, keepdims=True)
    )
    return (hidden, vision_output_gradient.astype(jnp.bfloat16))


def solution(mesh):
    in_specs = (
        P(("grp", "seq"), None),
        P(("grp", "seq"), None),
        P(("grp", "seq"), None),
        P(("grp", "seq")),
        P(),
        P("grp", "seq"),
        P(("grp", "seq"), None),
        P(),
        P(("grp", "seq"), None),
        P(("grp", "seq")),
        P(("grp", "seq")),
    )
    out_specs = (P(("grp", "seq"), None), P(("grp", "seq"), None))
    return jax.shard_map(body, mesh=mesh, in_specs=in_specs, out_specs=out_specs, check_vma=False)
```

profile of v0, /device:TPU:2, one launch (start us, length us, event | category | flops | bytes accessed | tf_op | source)
XLA Modules:
  0.0 489.1 jit_solution(493618908988585624)
XLA Ops:
  9.3 5.9 %all-to-all-start = ((bf16[256,8,160]{0,2,1:T(8,128)(2,1)}), bf16[256,8,160]{0,2,1:T(8,128)(2,1)S(1)}, u32[]{:S(2)}, u32[]{:S(2)}) async-start(bf16[256,8,160]{0,2,1:T(8,128)(2,1)} %bitcast.5), calls=%async_computation | async-start | bytes 1310720 | tf_op jit(solution)/shard_map/all_to_all | solution.py:58
  16.3 9.2 %all-to-all-done = bf16[256,8,160]{0,2,1:T(8,128)(2,1)S(1)} async-done(((bf16[256,8,160]{0,2,1:T(8,128)(2,1)}), bf16[256,8,160]{0,2,1:T(8,128)(2,1)S(1)}, u32[]{:S(2)}, u32[]{:S(2)}) %all-to-all-start) | async-done | bytes 655392 | tf_op jit(solution)/shard_map/all_to_all | solution.py:58
  25.5 4.9 %all-to-all-start.1 = ((bf16[256,8,160]{0,2,1:T(8,128)(2,1)}), bf16[256,8,160]{0,2,1:T(8,128)(2,1)S(1)}, u32[]{:S(2)}, u32[]{:S(2)}) async-start(bf16[256,8,160]{0,2,1:T(8,128)(2,1)} %bitcast.7), calls=%async_computation.1 | async-start | bytes 1310720 | tf_op jit(solution)/shard_map/all_to_all | solution.py:59
  31.5 9.2 %all-to-all-done.1 = bf16[256,8,160]{0,2,1:T(8,128)(2,1)S(1)} async-done(((bf16[256,8,160]{0,2,1:T(8,128)(2,1)}), bf16[256,8,160]{0,2,1:T(8,128)(2,1)S(1)}, u32[]{:S(2)}, u32[]{:S(2)}) %all-to-all-start.1) | async-done | bytes 655392 | tf_op jit(solution)/shard_map/all_to_all | solution.py:59
  40.7 4.9 %all-to-all-start.2 = ((bf16[256,8,160]{0,2,1:T(8,128)(2,1)}), bf16[256,8,160]{0,2,1:T(8,128)(2,1)S(1)}, u32[]{:S(2)}, u32[]{:S(2)}) async-start(bf16[256,8,160]{0,2,1:T(8,128)(2,1)} %bitcast.9), calls=%async_computation.2 | async-start | bytes 1310720 | tf_op jit(solution)/shard_map/all_to_all | solution.py:60
  45.6 12.6 %all-gather = s32[8,1,256]{2,1,0:T(1,128)S(1)} all-gather(s32[1,1,256]{2,1,0:T(1,128)S(1)} %bitcast.77), channel_id=1, replica_groups=mesh['grp'=32,'seq'=8] {'seq'}, dimensions={0}, use_global_device_ids=true | all-gather | bytes 9216 | tf_op jit(solution)/shard_map/all_gather | solution.py:62
  60.3 50.8 %while.10 = (s32[]{:T(128)}, bf16[4,512,160]{1,2,0:T(8,128)(2,1)}, s32[4]{0:T(128)S(1)}, s32[2048]{0:T(1024)S(1)}, bf16[2048,2,80]{0,2,1:T(8,128)(2,1)S(1)}, /*i...) while((s32[]{:T(128)}, bf16[4,512,160]{1,2,0:T(8,128)(2,1)}, ...), condition=%wide.region_3.4_spmd, body=%wide.region_0.3_spmd.sunk | while | flops 684804096 | bytes 20863664 | solution.py:40
  62.3 5.2 %fusion.53 = (f32[2,512]{1,0:T(2,128)S(1)}, f32[2,512,2048]{2,1,0:T(8,128)}) fusion(pred[512,2048]{1,0:T(8,128)(4,1)S(1)} %broadcast_compare_fusion.2, bf16[2048,2,80]{0,2,1:T(8,128)(2,1)S(1)} %get-tuple-element.142, bf16[2048,2,80]{0,2,1:T(8,128)(2,1)S(1)} %get-tuple-element.141, s32[]{:T(128)S(6)} %select_n.33), kind=kOutput, calls=%fused_computation.60.clone.1 | convolution fusion | flops 343934976 | bytes 10260484 | tf_op jit(solution)/shard_map/while/body/eval_jaxpr/sub | solution.py:36
  67.5 4.8 fusion.54
  75.0 5.2 %fusion.53 = (f32[2,512]{1,0:T(2,128)S(1)}, f32[2,512,2048]{2,1,0:T(8,128)}) fusion(pred[512,2048]{1,0:T(8,128)(4,1)S(1)} %broadcast_compare_fusion.2, bf16[2048,2,80]{0,2,1:T(8,128)(2,1)S(1)} %get-tuple-element.142, bf16[2048,2,80]{0,2,1:T(8,128)(2,1)S(1)} %get-tuple-element.141, s32[]{:T(128)S(6)} %select_n.33), kind=kOutput, calls=%fused_computation.60.clone.1 | convolution fusion | flops 343934976 | bytes 10260484 | tf_op jit(solution)/shard_map/while/body/eval_jaxpr/sub | solution.py:36
  80.2 4.8 fusion.54
  87.7 5.2 %fusion.53 = (f32[2,512]{1,0:T(2,128)S(1)}, f32[2,512,2048]{2,1,0:T(8,128)}) fusion(pred[512,2048]{1,0:T(8,128)(4,1)S(1)} %broadcast_compare_fusion.2, bf16[2048,2,80]{0,2,1:T(8,128)(2,1)S(1)} %get-tuple-element.142, bf16[2048,2,80]{0,2,1:T(8,128)(2,1)S(1)} %get-tuple-element.141, s32[]{:T(128)S(6)} %select_n.33), kind=kOutput, calls=%fused_computation.60.clone.1 | convolution fusion | flops 343934976 | bytes 10260484 | tf_op jit(solution)/shard_map/while/body/eval_jaxpr/sub | solution.py:36
  92.9 4.8 fusion.54
  100.4 5.2 %fusion.53 = (f32[2,512]{1,0:T(2,128)S(1)}, f32[2,512,2048]{2,1,0:T(8,128)}) fusion(pred[512,2048]{1,0:T(8,128)(4,1)S(1)} %broadcast_compare_fusion.2, bf16[2048,2,80]{0,2,1:T(8,128)(2,1)S(1)} %get-tuple-element.142, bf16[2048,2,80]{0,2,1:T(8,128)(2,1)S(1)} %get-tuple-element.141, s32[]{:T(128)S(6)} %select_n.33), kind=kOutput, calls=%fused_computation.60.clone.1 | convolution fusion | flops 343934976 | bytes 10260484 | tf_op jit(solution)/shard_map/while/body/eval_jaxpr/sub | solution.py:36
  105.6 4.8 fusion.54
  111.1 1.6 copy.45
  113.9 5.5 %all-to-all-start.3 = ((bf16[8,256,160]{1,2,0:T(8,128)(2,1)}), bf16[8,256,160]{1,2,0:T(8,128)(2,1)S(1)}, u32[]{:S(2)}, u32[]{:S(2)}) async-start(bf16[8,256,160]{1,2,0:T(8,128)(2,1)} %copy.46), calls=%async_computation.3 | async-start | bytes 1310720 | tf_op jit(solution)/shard_map/all_to_all | solution.py:64
  119.4 10.3 %all-to-all-done.3 = bf16[8,256,160]{1,2,0:T(8,128)(2,1)S(1)} async-done(((bf16[8,256,160]{1,2,0:T(8,128)(2,1)}), bf16[8,256,160]{1,2,0:T(8,128)(2,1)S(1)}, u32[]{:S(2)}, u32[]{:S(2)}) %all-to-all-start.3) | async-done | bytes 655392 | tf_op jit(solution)/shard_map/all_to_all | solution.py:64
  130.6 1.3 copy.55
  132.2 1.3 copy.54
  133.6 1.1 copy.47
  134.7 2.8 reshape.147
  137.5 2.7 multiply_convert_fusion.1
  141.0 38.6 %all-gather.4.cloned.1.call-done = bf16[512,5120]{1,0:T(8,128)(2,1)} async-done(((bf16[64,5120]{1,0:T(8,128)(2,1)}), bf16[512,5120]{1,0:T(8,128)(2,1)}) %all-gather.4.cloned.1.call-update) | async-done | bytes 5242896 | tf_op jit(solution)/shard_map/all_gather | solution.py:78
  179.6 112.7 %all-gather.6.cloned.1.call-done = bf16[5120,1024]{1,0:T(8,128)(2,1)} async-done(((bf16[160,1024]{1,0:T(8,128)(2,1)}), bf16[5120,1024]{1,0:T(8,128)(2,1)}) %all-gather.6.cloned.1.call-update) | async-done | bytes 10485776 | tf_op jit(solution)/shard_map/all_gather | solution.py:76
  292.3 10.6 %convolution_convert_fusion.1 = bf16[512,1024]{1,0:T(8,128)(2,1)} fusion(bf16[512,5120]{1,0:T(8,128)(2,1)} %all-gather.4.cloned.1.call-done, bf16[5120,1024]{1,0:T(8,128)(2,1)} %all-gather.6.cloned.1.call-done), kind=kOutput, calls=%fused_computation.37 | convolution fusion | flops 5369233408 | bytes 16777216 | tf_op jit(solution)/shard_map/dot_general | solution.py:77
  302.9 4.9 %all-to-all-start.4 = ((bf16[8,64,1024]{2,1,0:T(8,128)(2,1)}), bf16[8,64,1024]{2,1,0:T(8,128)(2,1)S(1)}, u32[]{:S(2)}, u32[]{:S(2)}) async-start(bf16[8,64,1024]{2,1,0:T(8,128)(2,1)} %bitcast.12), calls=%async_computation.4 | async-start | bytes 2097152 | tf_op jit(solution)/shard_map/all_to_all | solution.py:82
  307.9 14.5 %all-to-all-done.4 = bf16[8,64,1024]{2,1,0:T(8,128)(2,1)S(1)} async-done(((bf16[8,64,1024]{2,1,0:T(8,128)(2,1)}), bf16[8,64,1024]{2,1,0:T(8,128)(2,1)S(1)}, u32[]{:S(2)}, u32[]{:S(2)}) %all-to-all-start.4) | async-done | bytes 1048608 | tf_op jit(solution)/shard_map/all_to_all | solution.py:82
  322.4 2.3 scatter_custom_fusion
  324.7 1.5 all_to_all.103
  326.2 5.9 %all-to-all-start.5 = ((bf16[32,2,8192]{2,1,0:T(2,128)(2,1)}), bf16[32,2,8192]{2,1,0:T(2,128)(2,1)}, u32[]{:S(2)}, u32[]{:S(2)}) async-start(bf16[32,2,8192]{2,1,0:T(2,128)(2,1)} %all_to_all.103), calls=%async_computation.5 | async-start | bytes 2097152 | tf_op jit(solution)/shard_map/all_to_all | solution.py:84
  332.2 28.5 %all-to-all-done.5 = bf16[32,2,8192]{2,1,0:T(2,128)(2,1)} async-done(((bf16[32,2,8192]{2,1,0:T(2,128)(2,1)}), bf16[32,2,8192]{2,1,0:T(2,128)(2,1)}, u32[]{:S(2)}, u32[]{:S(2)}) %all-to-all-start.5) | async-done | bytes 1048608 | tf_op jit(solution)/shard_map/all_to_all | solution.py:84
  360.7 1.5 reshape.179
  362.2 3.3 scatter_fusion
  365.5 2.8 fusion.29
  368.3 2.5 fusion.27
  370.8 4.0 gather_fusion
  374.8 1.5 convert_element_type.70
  376.3 5.1 %all-to-all-start.6 = ((bf16[32,2,8192]{2,1,0:T(2,128)(2,1)}), bf16[32,2,8192]{2,1,0:T(2,128)(2,1)}, u32[]{:S(2)}, u32[]{:S(2)}) async-start(bf16[32,2,8192]{2,1,0:T(2,128)(2,1)} %convert_element_type.70), calls=%async_computation.6 | async-start | bytes 2097152 | tf_op jit(solution)/shard_map/all_to_all | solution.py:93
  381.5 28.2 %all-to-all-done.6 = bf16[32,2,8192]{2,1,0:T(2,128)(2,1)} async-done(((bf16[32,2,8192]{2,1,0:T(2,128)(2,1)}), bf16[32,2,8192]{2,1,0:T(2,128)(2,1)}, u32[]{:S(2)}, u32[]{:S(2)}) %all-to-all-start.6) | async-done | bytes 1048608 | tf_op jit(solution)/shard_map/all_to_all | solution.py:93
  409.7 1.5 all_to_all.107
  411.2 2.2 gather_fusion.1
  413.4 1.3 copy.57
  414.7 18.5 %all_to_all.120 = bf16[64,8,1024]{2,0,1:T(8,128)(2,1)S(1)} all-to-all(bf16[64,8,1024]{2,0,1:T(8,128)(2,1)S(1)} %bitcast.69), channel_id=1, replica_groups=mesh['grp'=32,'seq'=8] {'seq'}, dimensions={1} | all-to-all | bytes 2097152 | tf_op jit(solution)/shard_map/all_to_all | solution.py:95
  433.2 11.3 %convolution_convert_fusion = bf16[512,5120]{1,0:T(8,128)(2,1)} fusion(bf16[512,1024]{1,0:T(8,128)(2,1)S(1)} %bitcast.75, bf16[5120,1024]{1,0:T(8,128)(2,1)} %all-gather.6.cloned.1.call-done), kind=kOutput, calls=%fused_computation.24 | convolution fusion | flops 5371330560 | bytes 16777216 | tf_op jit(solution)/shard_map/dot_general | solution.py:97
  444.5 1.9 fusion.24
  446.4 32.4 %reduce-scatter.2.cloned.1.call-done = bf16[64,5120]{1,0:T(8,128)(2,1)} async-done(((bf16[512,5120]{1,0:T(8,128)(2,1)}), bf16[64,5120]{1,0:T(8,128)(2,1)}) %reduce-scatter.2.cloned.1.call-update) | async-done | bytes 655376 | tf_op jit(solution)/shard_map/reduce_scatter | solution.py:96
  478.9 1.5 reshape.149
  (85 shorter events, 20.0 us)
Async XLA Ops:
  7.2 1.1 copy-start.5
  8.3 6.9 %copy-start.6 = (bf16[256,1280]{1,0:T(8,128)(2,1)S(1)}, bf16[256,1280]{1,0:T(8,128)(2,1)}, u32[]{:S(2)}) copy-start(bf16[256,1280]{1,0:T(8,128)(2,1)} %param.14) | copy-start | bytes 1966084
  9.3 21.1 %copy-start.7 = (bf16[256,1280]{1,0:T(8,128)(2,1)S(1)}, bf16[256,1280]{1,0:T(8,128)(2,1)}, u32[]{:S(2)}) copy-start(bf16[256,1280]{1,0:T(8,128)(2,1)} %param.15) | copy-start | bytes 1966084
  9.3 16.2 %all-to-all-start = ((bf16[256,8,160]{0,2,1:T(8,128)(2,1)}), bf16[256,8,160]{0,2,1:T(8,128)(2,1)S(1)}, u32[]{:S(2)}, u32[]{:S(2)}) async-start(bf16[256,8,160]{0,2,1:T(8,128)(2,1)} %bitcast.5), calls=%async_computation | async-start | bytes 1310720 | tf_op jit(solution)/shard_map/all_to_all | solution.py:58
  16.3 29.4 %copy-start.10 = (s32[256]{0:T(256)S(1)}, s32[256]{0:T(256)}, u32[]{:S(2)}) copy-start(s32[256]{0:T(256)} %param.16) | copy-start | bytes 3076
  25.5 15.2 %all-to-all-start.1 = ((bf16[256,8,160]{0,2,1:T(8,128)(2,1)}), bf16[256,8,160]{0,2,1:T(8,128)(2,1)S(1)}, u32[]{:S(2)}, u32[]{:S(2)}) async-start(bf16[256,8,160]{0,2,1:T(8,128)(2,1)} %bitcast.7), calls=%async_computation.1 | async-start | bytes 1310720 | tf_op jit(solution)/shard_map/all_to_all | solution.py:59
  40.7 18.9 %all-to-all-start.2 = ((bf16[256,8,160]{0,2,1:T(8,128)(2,1)}), bf16[256,8,160]{0,2,1:T(8,128)(2,1)S(1)}, u32[]{:S(2)}, u32[]{:S(2)}) async-start(bf16[256,8,160]{0,2,1:T(8,128)(2,1)} %bitcast.9), calls=%async_computation.2 | async-start | bytes 1310720 | tf_op jit(solution)/shard_map/all_to_all | solution.py:60
  112.7 6.7 %copy-start.9 = (f32[1280]{0:T(1024)S(1)}, f32[1280]{0:T(1024)}, u32[]{:S(2)}) copy-start(f32[1280]{0:T(1024)} %param.17) | copy-start | bytes 15364
  113.9 15.8 %all-to-all-start.3 = ((bf16[8,256,160]{1,2,0:T(8,128)(2,1)}), bf16[8,256,160]{1,2,0:T(8,128)(2,1)S(1)}, u32[]{:S(2)}, u32[]{:S(2)}) async-start(bf16[8,256,160]{1,2,0:T(8,128)(2,1)} %copy.46), calls=%async_computation.3 | async-start | bytes 1310720 | tf_op jit(solution)/shard_map/all_to_all | solution.py:64
  119.4 60.2 %all-gather.4.cloned.1.call-start = ((), (), s32[]{:S(2)}) async-start(), calls=%async_computation.9 | async-start | bytes 5898240 | tf_op jit(solution)/shard_map/all_gather | solution.py:78
  129.7 3.7 copy-start.1
  134.7 2.8 copy-start.4
  140.2 152.1 %all-gather.6.cloned.1.call-start = ((), (), s32[]{:S(2)}) async-start(), calls=%async_computation.10 | async-start | bytes 10813440 | tf_op jit(solution)/shard_map/all_gather | solution.py:76
  302.9 5.0 %copy-start.11 = (s32[64]{0:T(128)S(1)}, s32[64]{0:T(128)}, u32[]{:S(2)}) copy-start(s32[64]{0:T(128)} %param.22) | copy-start | bytes 772
  302.9 19.5 %all-to-all-start.4 = ((bf16[8,64,1024]{2,1,0:T(8,128)(2,1)}), bf16[8,64,1024]{2,1,0:T(8,128)(2,1)S(1)}, u32[]{:S(2)}, u32[]{:S(2)}) async-start(bf16[8,64,1024]{2,1,0:T(8,128)(2,1)} %bitcast.12), calls=%async_computation.4 | async-start | bytes 2097152 | tf_op jit(solution)/shard_map/all_to_all | solution.py:82
  324.7 7.4 %copy-start.12 = (s32[64]{0:T(128)S(1)}, s32[64]{0:T(128)}, u32[]{:S(2)}) copy-start(s32[64]{0:T(128)} %param.23) | copy-start | bytes 772
  326.2 35.9 %copy-start = (bf16[128,8192]{1,0:T(8,128)(2,1)S(1)}, bf16[128,8192]{1,0:T(8,128)(2,1)}, u32[]{:S(2)}) copy-start(bf16[128,8192]{1,0:T(8,128)(2,1)} %param.19) | copy-start | bytes 6291460
  326.2 34.4 %all-to-all-start.5 = ((bf16[32,2,8192]{2,1,0:T(2,128)(2,1)}), bf16[32,2,8192]{2,1,0:T(2,128)(2,1)}, u32[]{:S(2)}, u32[]{:S(2)}) async-start(bf16[32,2,8192]{2,1,0:T(2,128)(2,1)} %all_to_all.103), calls=%async_computation.5 | async-start | bytes 2097152 | tf_op jit(solution)/shard_map/all_to_all | solution.py:84
  362.1 3.3 copy-start.8
  365.5 2.8 copy-start.3
  376.3 33.4 %all-to-all-start.6 = ((bf16[32,2,8192]{2,1,0:T(2,128)(2,1)}), bf16[32,2,8192]{2,1,0:T(2,128)(2,1)}, u32[]{:S(2)}, u32[]{:S(2)}) async-start(bf16[32,2,8192]{2,1,0:T(2,128)(2,1)} %convert_element_type.70), calls=%async_computation.6 | async-start | bytes 2097152 | tf_op jit(solution)/shard_map/all_to_all | solution.py:93
  381.5 97.4 %reduce-scatter.2.cloned.1.call-start = ((), (), s32[]{:S(2)}) async-start(), calls=%async_computation.11 | async-start | bytes 5898240 | tf_op jit(solution)/shard_map/reduce_scatter | solution.py:96
  446.4 34.3 %copy-start.2 = (bf16[8,256,160]{1,2,0:T(8,128)(2,1)S(1)}, bf16[8,256,160]{1,2,0:T(8,128)(2,1)}, u32[]{:S(2)}) copy-start(bf16[8,256,160]{1,2,0:T(8,128)(2,1)} %copy-done.1) | copy-start | bytes 1966084
Sparse Core Ops, SparseCore 0:
  140.4 39.1 all-gather.3
  182.2 110.0 all-gather.5
  444.6 34.1 reduce-scatter.1
where the time goes:
time: 494 us; the launch traced here: 489 us
  waiting for transfers between devices  284 us (57%)
  matrix products  61.9 us (13%)
  local copies, waits for them, and re-layouts  43.8 us (9%)
  starting transfers between devices  37.2 us (8%)
  blocking collectives  31.2 us (6%)
  between operations  14.1 us (3%)
  other arithmetic  13.9 us (3%)
    all_gather x1, waiting for transfers between devices, body(): w_columns = lax.all_gather(merge_weight, 'grp', axis=0, tiled=True)  113 us
    all_gather x1, waiting for transfers between devices, body(): lax.all_gather(merged_patches, 'seq', axis=0, tiled=True)  38.6 us
    reduce_scatter x1, waiting for transfers between devices, body(): lax.psum_scatter(lax.dot_general(returned, w_columns, (((1,), (1,)), ((),...  32.4 us
    all_to_all x1, waiting for transfers between devices, body(): lax.all_to_all(slotted, 'grp', split_axis=0, concat_axis=0, tiled=True)  28.5 us
    all_to_all x1, waiting for transfers between devices, body(): lax.all_to_all(back_rows, 'grp', split_axis=0, concat_axis=0, tiled=True)  28.2 us
    sub x4, matrix products, one_block(): probs = jax.nn.softmax(scores, axis=-1).astype(jnp.bfloat16)  20.7 us
    dot_general x4, matrix products, one_block(): jnp.einsum('hqk,khd->qhd', probs, v_three, preferred_element_type=jnp.flo...  19.4 us
    all_to_all x1, blocking collectives, body(): lax.all_to_all(natural_grads, 'seq', split_axis=1, concat_axis=0, tiled=T...  18.5 us
  transfers between devices with their start and end apart: 10, of which 9 were waited for; matrix products, arithmetic and copies ran while one was open for 1% of the time, Pallas kernels for 0%

commit v1 on v0

v1 whole, which is shorter than its diff:
```python
import functools

import jax
import jax.numpy as jnp
from jax import lax
from jax.experimental import pallas as pl
from jax.experimental.pallas import tpu as pltpu
from jax.sharding import PartitionSpec as P

VISION_WIDTH = 1280
HEAD_DIM = 80
MERGER_FEATURES = 5120
ROWS = 64
HALF = 640
EPS = 1e-06
NT = (((1,), (1,)), ((), ()))
F32 = jnp.float32
BF16 = jnp.bfloat16
LOG2E = 1.4426950408889634
VMEM = pl.BlockSpec(memory_space=pltpu.VMEM)
PARAMS = pltpu.CompilerParams(vmem_limit_bytes=48 * 2**20)


def iota(shape, axis):
    return lax.broadcasted_iota(jnp.int32, shape, axis)


def eye(n):
    return (iota((n, n), 0) == iota((n, n), 1)).astype(F32).astype(BF16)


def mm(a, b):
    return jnp.dot(a, b, preferred_element_type=F32)


def mm_nt(a, b):
    return lax.dot_general(a, b, NT, preferred_element_type=F32)


def onehot(mask):
    return mask.astype(F32).astype(BF16)


def block_of_granule(rho):
    g, half, i, p = rho // 16, rho // 8 % 2, rho // 4 % 2, rho % 4
    return (p * 2 + half) * 64 + g * 2 + i


def split_heads(q_ref, k_ref, v_ref, ids_ref, out_ref):
    one = eye(256)
    for t, ref in enumerate((q_ref, k_ref, v_ref)):
        for f in range(5):
            block = mm_nt(one, ref[:, 256 * f : 256 * f + 256]).astype(BF16)
            lower = 256 * f
            while lower < 256 * f + 256:
                dev = lower // 160
                upper = min(160 * (dev + 1), 256 * f + 256)
                out_ref[dev, 160 * t + lower - 160 * dev : 160 * t + upper - 160 * dev, :] = block[
                    lower - 256 * f : upper - 256 * f, :
                ]
                lower = upper
    ids = ids_ref[...]
    rows = jnp.where(iota((16, 256), 0) % 2 == 0, ids // 16, ids % 16)
    rows = rows.astype(F32).astype(BF16)
    for dev in range(8):
        out_ref[dev, 480:496, :] = rows


def attention(x_ref, o_ref, k_scr, idk_scr, s_scr):
    one = eye(256)
    scale = HEAD_DIM ** (-0.5) * LOG2E
    first, last, id_rows = [], [], []
    for j in range(8):
        for h in range(2):
            k_scr[j, h] = mm_nt(one, x_ref[j, 160 + 80 * h : 240 + 80 * h, :]).astype(BF16)
        parts = x_ref[j, 480:496, :]
        cols = mm_nt(one, parts)
        idk_scr[j] = jnp.broadcast_to(cols[:, 0:1] * 16.0 + cols[:, 1:2], (256, 128))
        parts = parts.astype(F32)
        row = parts[0:1] * 16.0 + parts[1:2]
        first.append(jnp.min(row))
        last.append(jnp.max(row))
    for i in range(8):
        parts = x_ref[i, 480:496, :].astype(F32)
        idq = parts[0:1] * 16.0 + parts[1:2]
        lo, hi = jnp.int32(0), jnp.int32(8)
        for j in range(8):
            if j < i:
                lo = lo + jnp.where(last[j] < first[i], 1, 0)
            if j > i:
                hi = hi - jnp.where(first[j] > last[i], 1, 0)

        def scores(j, m):
            idk = idk_scr[j]
            same = jnp.concatenate([idk, idk], axis=1) == idq
            new = []
            for h in range(2):
                s = mm(k_scr[j, h], x_ref[i, 80 * h : 80 * h + 80, :])
                s = jnp.where(same, s, -1e30)
                s_scr[h, j] = s
                new.append(jnp.maximum(m[h], jnp.max(s.reshape(32, 8, 256), axis=0)))
            return tuple(new)

        m = lax.fori_loop(lo, hi, scores, (jnp.full((8, 256), -1e30, F32),) * 2)
        top = [jnp.max(m[h], axis=0, keepdims=True) for h in range(2)]

        def weighted(j, carry):
            new = []
            for h in range(2):
                acc, total = carry[h]
                p = jnp.exp2((s_scr[h, j] - top[h]) * scale)
                total = total + jnp.sum(p.reshape(32, 8, 256), axis=0)
                acc = acc + mm(x_ref[j, 320 + 80 * h : 400 + 80 * h, :], p.astype(BF16))
                new.append((acc, total))
            return tuple(new)

        zero = (jnp.zeros((HEAD_DIM, 256), F32), jnp.zeros((8, 256), F32))
        done = lax.fori_loop(lo, hi, weighted, (zero, zero))
        for h in range(2):
            acc, total = done[h]
            total = jnp.sum(total, axis=0, keepdims=True)
            o_ref[i, 80 * h : 80 * h + 80, :] = (acc / total).astype(BF16)


def normalize(attn_t, one):
    x = jnp.concatenate([mm_nt(one, attn_t[256 * f : 256 * f + 256, :]) for f in range(5)], axis=1)
    x = x - jnp.mean(x, axis=1, keepdims=True)
    rstd = lax.rsqrt(jnp.mean(x * x, axis=1, keepdims=True) + EPS)
    return x * rstd, rstd


def merge(attn_ref, gain_ref, target_ref, out_ref):
    xhat, _ = normalize(attn_ref[...].reshape(VISION_WIDTH, 256), eye(256))
    merged = (xhat * gain_ref[...]).astype(BF16)
    stacked = jnp.concatenate([merged[:, :HALF], merged[:, HALF:]], axis=0)
    pick = onehot(iota((512, 512), 0) == target_ref[...])
    out_ref[...] = mm(pick, stacked).astype(BF16).reshape(32, 16, HALF)


def to_blocks(x_ref, out_ref):
    pick = onehot(iota((512, 512), 0) == block_of_granule(iota((512, 512), 1)))
    out_ref[...] = mm(pick, x_ref[...].reshape(512, HALF)).astype(BF16).reshape(8, ROWS, HALF)


def to_granules(x_ref, out_ref):
    pick = onehot(block_of_granule(iota((512, 512), 0)) == iota((512, 512), 1))
    out_ref[...] = mm(pick, x_ref[...].reshape(512, HALF)).astype(BF16).reshape(32, 16, HALF)


def project(a_ref, w_ref, out_ref):
    total = jnp.zeros((512, 256), F32)
    for b in range(8):
        total = total + mm(a_ref[:, b].reshape(512, HALF), w_ref[HALF * b : HALF * b + HALF, :])
    out_ref[...] = total.astype(BF16).reshape(8, ROWS, 256)


def project_back(a_ref, w_ref, out_ref):
    out_ref[...] = mm_nt(a_ref[...].reshape(512, 1024), w_ref[...]).astype(BF16).reshape(8, 1, ROWS, HALF)


def token_norm(vis_ref, text_ref, cot_ref, gain_ref, pos_ref, posc_ref, hid_ref, back_ref, inp_scr):
    place = onehot(iota((128, ROWS), 0) == pos_ref[...])
    pick = onehot(iota((ROWS, 128), 1) == posc_ref[...])
    taken = jnp.sum(place.astype(F32), axis=1, keepdims=True) > 0.5
    squares = jnp.zeros((128, 1), F32)
    products = jnp.zeros((128, 1), F32)
    for c in range(8):
        cols = slice(1024 * c, 1024 * c + 1024)
        inp = jnp.where(taken, mm(place, vis_ref[c]), text_ref[:, cols].astype(F32))
        inp_scr[:, cols] = inp
        squares = squares + jnp.sum(inp * inp, axis=1, keepdims=True)
        gy = cot_ref[:, cols].astype(F32) * gain_ref[:, cols]
        products = products + jnp.sum(gy * inp, axis=1, keepdims=True)
    r = lax.rsqrt(squares / 8192.0 + EPS)
    slope = r * r * (products / 8192.0)
    for c in range(8):
        cols = slice(1024 * c, 1024 * c + 1024)
        inp = inp_scr[:, cols]
        gain = gain_ref[:, cols]
        hid_ref[:, cols] = (inp * r * gain).astype(BF16)
        gy = cot_ref[:, cols].astype(F32) * gain
        grads = (r * (gy - inp * slope)).astype(BF16)
        back_ref[c] = mm(pick, grads).astype(BF16)


def patch_grads(attn_ref, g_ref, gain_ref, target_ref, out_ref):
    xhat, rstd = normalize(attn_ref[...].reshape(VISION_WIDTH, 256), eye(256))
    pick = onehot(iota((512, 512), 1) == target_ref[...])
    grads = mm(pick, g_ref[...].reshape(512, HALF))
    gy = jnp.concatenate([grads[:256], grads[256:]], axis=1) * gain_ref[...]
    mean = jnp.mean(gy, axis=1, keepdims=True)
    along = jnp.mean(gy * xhat, axis=1, keepdims=True)
    out_ref[...] = (rstd * (gy - mean - xhat * along)).astype(BF16)


def local(kernel, shape, dtype, n_in, scratch=(), name=None):
    many = isinstance(shape, list)
    out = [jax.ShapeDtypeStruct(s, dtype) for s in shape] if many else jax.ShapeDtypeStruct(shape, dtype)
    return pl.pallas_call(
        kernel,
        out_shape=out,
        in_specs=[VMEM] * n_in,
        out_specs=[VMEM] * len(shape) if many else VMEM,
        scratch_shapes=list(scratch),
        compiler_params=PARAMS,
        name=name,
    )


def body(
    queries,
    key_rows,
    values,
    segment_ids,
    merger_norm_gain,
    merge_weight,
    text_rows,
    token_gain,
    cotangent,
    send_slot,
    place_pos,
):
    w = lax.all_gather(merge_weight, "grp", axis=0, tiled=True)
    gain = merger_norm_gain.reshape(1, VISION_WIDTH)
    slot = jnp.tile(jnp.repeat(send_slot, 4), 2)
    kappa = jnp.arange(512, dtype=jnp.int32)
    target = slot // 2 * 16 + kappa // 256 * 8 + slot % 2 * 4 + kappa % 4

    x = local(split_heads, (8, 496, 256), BF16, 4, name="split_heads")(
        queries, key_rows, values, segment_ids.reshape(1, 256)
    )
    x = lax.all_to_all(x, "seq", split_axis=0, concat_axis=0, tiled=True)
    o = local(
        attention,
        (8, 160, 256),
        BF16,
        1,
        [
            pltpu.VMEM((8, 2, 256, HEAD_DIM), BF16),
            pltpu.VMEM((8, 256, 128), F32),
            pltpu.VMEM((2, 8, 256, 256), F32),
        ],
        name="attention",
    )(x)
    attn = lax.all_to_all(o, "seq", split_axis=0, concat_axis=0, tiled=True)
    routed = local(merge, (32, 16, HALF), BF16, 3, name="merge")(attn, gain, target.reshape(1, 512))
    routed = lax.all_to_all(routed, "grp", split_axis=0, concat_axis=0, tiled=True)
    blocks = local(to_blocks, (8, ROWS, HALF), BF16, 1, name="to_blocks")(routed)
    gathered = lax.all_gather(blocks, "seq", axis=0)
    vision = pl.pallas_call(
        project,
        grid=(4,),
        out_shape=jax.ShapeDtypeStruct((8, ROWS, 1024), BF16),
        in_specs=[
            pl.BlockSpec((8, 8, ROWS, HALF), lambda n: (0, 0, 0, 0)),
            pl.BlockSpec((MERGER_FEATURES, 256), lambda n: (0, n)),
        ],
        out_specs=pl.BlockSpec((8, ROWS, 256), lambda n: (0, 0, n)),
        compiler_params=PARAMS,
        name="project",
    )(gathered, w)
    vision = lax.all_to_all(vision, "seq", split_axis=0, concat_axis=0, tiled=True)
    hidden, back = local(
        token_norm, [(128, 8192), (8, ROWS, 1024)], BF16, 6, [pltpu.VMEM((128, 8192), F32)], name="token_norm"
    )(
        vision,
        text_rows,
        cotangent,
        token_gain.reshape(1, 8192),
        place_pos.reshape(1, ROWS),
        place_pos.reshape(ROWS, 1),
    )
    back = lax.all_to_all(back, "seq", split_axis=0, concat_axis=0, tiled=True)
    terms = pl.pallas_call(
        project_back,
        grid=(8,),
        out_shape=jax.ShapeDtypeStruct((8, 8, ROWS, HALF), BF16),
        in_specs=[
            pl.BlockSpec((8, ROWS, 1024), lambda n: (0, 0, 0)),
            pl.BlockSpec((HALF, 1024), lambda n: (n, 0)),
        ],
        out_specs=pl.BlockSpec((8, 1, ROWS, HALF), lambda n: (0, n, 0, 0)),
        compiler_params=PARAMS,
        name="project_back",
    )(back, w)
    summed = lax.psum_scatter(terms.reshape(8 * 512, HALF), "seq", scatter_dimension=0, tiled=True)
    granules = local(to_granules, (32, 16, HALF), BF16, 1, name="to_granules")(summed.reshape(8, ROWS, HALF))
    granules = lax.all_to_all(granules, "grp", split_axis=0, concat_axis=0, tiled=True)
    vision_output_gradient = local(patch_grads, (256, VISION_WIDTH), BF16, 4, name="patch_grads")(
        attn, granules, gain, target.reshape(512, 1)
    )
    return hidden, vision_output_gradient


def solution(mesh):
    in_specs = (
        P(("grp", "seq"), None),
        P(("grp", "seq"), None),
        P(("grp", "seq"), None),
        P(("grp", "seq")),
        P(),
        P("grp", "seq"),
        P(("grp", "seq"), None),
        P(),
        P(("grp", "seq"), None),
        P(("grp", "seq")),
        P(("grp", "seq")),
    )
    out_specs = (P(("grp", "seq"), None), P(("grp", "seq"), None))
    return jax.shard_map(body, mesh=mesh, in_specs=in_specs, out_specs=out_specs, check_vma=False)
```

time: 494 us -> 402 us (0.81)
  matrix products: 61.9 us -> 0 us
  waiting for transfers between devices: 284 us -> 225 us
  Pallas kernels: 0 us -> 52.9 us
  blocking collectives: 31.2 us -> 80.1 us
  local copies, waits for them, and re-layouts: 43.8 us -> 7.06 us
  starting transfers between devices: 37.2 us -> 19.8 us
  other arithmetic: 13.9 us -> 0.33 us
    all_to_all x1 -> x3, blocking collectives: 18.5 us -> 80.1 us  [the longest x1 31.6 us: body(): lax.all_to_all(routed, 'grp', split_axis=0, concat_axis=0, tiled=True)]
    all_to_all x7 -> x3, waiting for transfers between devices: 100 us -> 44.2 us  [the longest x1 19.8 us: body(): lax.all_to_all(granules, 'grp', split_axis=0, concat_axis=0, tiled=True)]
    pallas_call x0 -> x9, Pallas kernels: none -> 52.9 us  [the longest x1 17.1 us: body(): local(attention, (8, 160, 256), BF16, 1, [pltpu.VMEM((8, 2, 256, HEAD_DIM...]
    dot_general x6 -> x0, matrix products: 41.2 us -> none  [the longest x4 19.4 us: one_block(): jnp.einsum('hqk,khd->qhd', probs, v_three, preferred_element_type=jnp.flo...]
    sub x4 -> x0, matrix products: 20.7 us -> none  [one_block(): probs = jax.nn.softmax(scores, axis=-1).astype(jnp.bfloat16)]
    all_to_all x7 -> x3, starting transfers between devices: 37.1 us -> 19.7 us  [the longest x1 9.85 us: body(): lax.all_to_all(granules, 'grp', split_axis=0, concat_axis=0, tiled=True)]
    all_gather x1 -> x0, blocking collectives: 12.6 us -> none  [body(): images = lax.all_gather(segment_ids, 'seq', axis=0, tiled=True)]
    all_to_all x10 -> x0, local copies, waits for them, and re-layouts: 8.02 us -> none  [the longest x2 2.96 us: body(): lax.all_to_all(slotted, 'grp', split_axis=0, concat_axis=0, tiled=True)]
  transfers between devices with their start and end apart: 10 -> 6, of which waited for: 9 -> 6; matrix products, arithmetic and copies ran while one was open for 1% -> 0% of each run, Pallas kernels for 0% -> 0%
where the time goes in v1:
time: 402 us; the launch traced here: 399 us
  waiting for transfers between devices  225 us (56%)
  blocking collectives  80.1 us (20%)
  Pallas kernels  52.9 us (13%)
  starting transfers between devices  19.8 us (5%)
  between operations  13.8 us (3%)
  local copies, waits for them, and re-layouts  7.06 us (2%)
    all_gather x1, waiting for transfers between devices, body(): w = lax.all_gather(merge_weight, 'grp', axis=0, tiled=True)  113 us
    reduce_scatter x1, waiting for transfers between devices, body(): lax.psum_scatter(terms.reshape(8 * 512, HALF), 'seq', scatter_dimension=0...  35.1 us
    all_gather x1, waiting for transfers between devices, body(): gathered = lax.all_gather(blocks, 'seq', axis=0)  32.7 us
    all_to_all x1, blocking collectives, body(): lax.all_to_all(routed, 'grp', split_axis=0, concat_axis=0, tiled=True)  31.6 us
    all_to_all x1, blocking collectives, body(): x = lax.all_to_all(x, 'seq', split_axis=0, concat_axis=0, tiled=True)  30 us
    all_to_all x1, waiting for transfers between devices, body(): lax.all_to_all(granules, 'grp', split_axis=0, concat_axis=0, tiled=True)  19.8 us
    all_to_all x1, blocking collectives, body(): back = lax.all_to_all(back, 'seq', split_axis=0, concat_axis=0, tiled=True)  18.5 us
    pallas_call x1, Pallas kernels, body(): local(attention, (8, 160, 256), BF16, 1, [pltpu.VMEM((8, 2, 256, HEAD_DIM...  17.1 us
  transfers between devices with their start and end apart: 6, of which 6 were waited for; matrix products, arithmetic and copies ran while one was open for 0% of the time, Pallas kernels for 0%

profile of v1, /device:TPU:2, one launch (start us, length us, event | category | flops | bytes accessed | tf_op | source)
XLA Modules:
  0.0 399.5 jit_solution(12925202056015393824)
XLA Ops:
  7.2 0.0 copy-start.1
  7.2 1.1 copy-done.1
  8.3 0.0 copy-start.2
  8.3 1.1 copy-done.2
  9.3 0.0 copy-start.3
  9.3 1.1 copy-done.3
  10.4 0.0 copy-start.7
  10.4 0.7 copy-done.7
  11.1 0.7 split_heads.1
  11.8 30.0 %all_to_all.30.x_ref = bf16[8,496,256]{2,1,0:T(8,128)(2,1)S(1)} all-to-all(bf16[8,496,256]{2,1,0:T(8,128)(2,1)S(1)} %split_heads.1), channel_id=1, replica_groups=mesh['grp'=32,'seq'=8] {'seq'}, dimensions={0} | all-to-all | bytes 4063232 | tf_op jit(solution)/shard_map/all_to_all | solution.py:232
  41.9 0.0 copy-start.8
  41.9 0.0 copy-start.9
  41.9 17.1 %attention.1 = bf16[8,160,256]{2,1,0:T(8,128)(2,1)} custom-call(bf16[8,496,256]{2,1,0:T(8,128)(2,1)S(1)} %all_to_all.30.x_ref), custom_call_target="tpu_custom_call" | custom-call | tf_op jit(solution)/shard_map/attention/pallas_call | solution.py:233
  59.0 4.9 %all-to-all-start.1 = ((bf16[8,160,256]{2,1,0:T(8,128)(2,1)}), bf16[8,160,256]{2,1,0:T(8,128)(2,1)S(1)}, u32[]{:S(2)}, u32[]{:S(2)}) async-start(bf16[8,160,256]{2,1,0:T(8,128)(2,1)} %attention.1), calls=%async_computation.1 | async-start | bytes 1310720 | tf_op jit(solution)/shard_map/all_to_all | solution.py:245
  63.9 0.0 all-gather.6.cloned.1.call-start
  63.9 0.0 copy-done.8
  63.9 0.0 copy-done.9
  63.9 0.1 broadcast_in_dim.3
  64.0 0.1 tile.12
  64.2 10.1 %all-to-all-done.1.attn_ref = bf16[8,160,256]{2,1,0:T(8,128)(2,1)S(1)} async-done(((bf16[8,160,256]{2,1,0:T(8,128)(2,1)}), bf16[8,160,256]{2,1,0:T(8,128)(2,1)S(1)}, u32[]{:S(2)}, u32[]{:S(2)}) %all-to-all-start.1) | async-done | bytes 655392 | tf_op jit(solution)/shard_map/all_to_all | solution.py:245
  74.2 1.3 merge.1
  75.5 31.6 %all_to_all.31.x_ref = bf16[32,16,640]{2,1,0:T(8,128)(2,1)S(1)} all-to-all(bf16[32,16,640]{2,1,0:T(8,128)(2,1)S(1)} %merge.1), channel_id=1, replica_groups=mesh['grp'=32,'seq'=8] {'grp'}, dimensions={0} | all-to-all | bytes 1310720 | tf_op jit(solution)/shard_map/all_to_all | solution.py:247
  107.1 1.4 to_blocks.1
  108.5 0.0 all-gather.6.cloned.1.call-update
  108.5 0.0 all-gather.4.cloned.1.call-start
  108.5 0.7 all-gather.4.cloned.1.call-update
  109.2 32.7 %all-gather.6.cloned.1.call-done = bf16[64,64,640]{2,1,0:T(8,128)(2,1)} async-done(((bf16[8,64,640]{2,1,0:T(8,128)(2,1)}), bf16[64,64,640]{2,1,0:T(8,128)(2,1)}) %all-gather.6.cloned.1.call-update) | async-done | bytes 5242896 | tf_op jit(solution)/shard_map/all_gather | solution.py:249
  142.0 112.7 %all-gather.4.cloned.1.call-done.w_ref = bf16[5120,1024]{1,0:T(8,128)(2,1)} async-done(((bf16[160,1024]{1,0:T(8,128)(2,1)}), bf16[5120,1024]{1,0:T(8,128)(2,1)}) %all-gather.4.cloned.1.call-update) | async-done | bytes 10485776 | tf_op jit(solution)/shard_map/all_gather | solution.py:223
  254.7 11.2 %project.1 = bf16[8,64,1024]{2,1,0:T(8,128)(2,1)} custom-call(bf16[8,8,64,640]{3,2,1,0:T(8,128)(2,1)} %bitcast.40, bf16[5120,1024]{1,0:T(8,128)(2,1)} %all-gather.4.cloned.1.call-done.w_ref), custom_call_target="tpu_custom_call" | custom-call | tf_op jit(solution)/shard_map/project/pallas_call | solution.py:250
  265.9 4.9 %all-to-all-start.3 = ((bf16[8,64,1024]{2,1,0:T(8,128)(2,1)}), bf16[8,64,1024]{2,1,0:T(8,128)(2,1)S(1)}, u32[]{:S(2)}, u32[]{:S(2)}) async-start(bf16[8,64,1024]{2,1,0:T(8,128)(2,1)} %project.1), calls=%async_computation.3 | async-start | bytes 2097152 | tf_op jit(solution)/shard_map/all_to_all | solution.py:262
  270.8 0.0 reduce-scatter.2.cloned.1.call-start
  270.8 0.0 copy-done.6
  270.8 0.1 copy.24.posc_ref
  270.9 14.4 %all-to-all-done.3.vis_ref = bf16[8,64,1024]{2,1,0:T(8,128)(2,1)S(1)} async-done(((bf16[8,64,1024]{2,1,0:T(8,128)(2,1)}), bf16[8,64,1024]{2,1,0:T(8,128)(2,1)S(1)}, u32[]{:S(2)}, u32[]{:S(2)}) %all-to-all-start.3) | async-done | bytes 1048608 | tf_op jit(solution)/shard_map/all_to_all | solution.py:262
  285.3 0.0 copy-done.5
  285.3 1.6 copy-done
  286.9 5.6 %token_norm.1 = (bf16[128,8192]{1,0:T(8,128)(2,1)}, bf16[8,64,1024]{2,1,0:T(8,128)(2,1)S(1)}) custom-call(bf16[8,64,1024]{2,1,0:T(8,128)(2,1)S(1)} %all-to-all-done.3.vis_ref, bf16[128,8192]{1,0:T(8,128)(2,1)S(1)} %copy-done, bf16[128,8192]{1,0:T(8,128)(2,1)} %cot_ref.1, f32[1,8192]{1,0:T(1,128)S(1)} %bitcast.35, s32[1,64]{1,0:T(1,128)S(1)} %bitcast.37, ...), custom_call_target="tpu_custom_call" | custom-call | tf_op jit(solution)/shard_map/token_norm/pallas_call | solution.py:263
  292.5 18.5 %all_to_all.32.a_ref = bf16[8,64,1024]{2,1,0:T(8,128)(2,1)S(1)} all-to-all(bf16[8,64,1024]{2,1,0:T(8,128)(2,1)S(1)} %get-tuple-element.5), channel_id=1, replica_groups=mesh['grp'=32,'seq'=8] {'seq'}, dimensions={0} | all-to-all | bytes 2097152 | tf_op jit(solution)/shard_map/all_to_all | solution.py:273
  311.0 12.3 %project_back.1 = bf16[8,8,64,640]{3,2,1,0:T(8,128)(2,1)} custom-call(bf16[8,64,1024]{2,1,0:T(8,128)(2,1)S(1)} %all_to_all.32.a_ref, bf16[5120,1024]{1,0:T(8,128)(2,1)} %all-gather.4.cloned.1.call-done.w_ref), custom_call_target="tpu_custom_call" | custom-call | tf_op jit(solution)/shard_map/project_back/pallas_call | solution.py:274
  323.2 0.0 reduce-scatter.2.cloned.1.call-update
  323.3 35.1 %reduce-scatter.2.cloned.1.call-done = bf16[512,640]{1,0:T(8,128)(2,1)} async-done(((bf16[4096,640]{1,0:T(8,128)(2,1)}), bf16[512,640]{1,0:T(8,128)(2,1)}) %reduce-scatter.2.cloned.1.call-update) | async-done | bytes 655376 | tf_op jit(solution)/shard_map/reduce_scatter | solution.py:286
  358.4 1.1 copy-done.4
  359.4 1.5 to_granules.1
  360.9 9.8 %all-to-all-start.5 = ((bf16[32,16,640]{2,1,0:T(8,128)(2,1)}), bf16[32,16,640]{2,1,0:T(8,128)(2,1)S(1)}, u32[]{:S(2)}, u32[]{:S(2)}) async-start(bf16[32,16,640]{2,1,0:T(8,128)(2,1)} %to_granules.1), calls=%async_computation.6 | async-start | bytes 1310720 | tf_op jit(solution)/shard_map/all_to_all | solution.py:288
  370.8 0.1 copy.32
  370.9 0.3 fusion.3.target_ref
  371.2 19.8 %all-to-all-done.5.g_ref = bf16[32,16,640]{2,1,0:T(8,128)(2,1)S(1)} async-done(((bf16[32,16,640]{2,1,0:T(8,128)(2,1)}), bf16[32,16,640]{2,1,0:T(8,128)(2,1)S(1)}, u32[]{:S(2)}, u32[]{:S(2)}) %all-to-all-start.5) | async-done | bytes 655392 | tf_op jit(solution)/shard_map/all_to_all | solution.py:288
  391.0 2.0 patch_grads.1
  (8 shorter events, 0.0 us)
Async XLA Ops:
  7.2 1.1 copy-start.1
  8.3 1.1 copy-start.2
  9.3 1.1 copy-start.3
  10.4 0.7 copy-start.7
  41.9 22.0 %copy-start.8 = (f32[1280]{0:T(1024)S(1)}, f32[1280]{0:T(1024)}, u32[]{:S(2)}) copy-start(f32[1280]{0:T(1024)} %param.15) | copy-start | bytes 15364
  41.9 22.1 %copy-start.9 = (s32[64]{0:T(128)S(1)}, s32[64]{0:T(128)}, u32[]{:S(2)}) copy-start(s32[64]{0:T(128)} %param.20) | copy-start | bytes 772
  59.0 15.3 %all-to-all-start.1 = ((bf16[8,160,256]{2,1,0:T(8,128)(2,1)}), bf16[8,160,256]{2,1,0:T(8,128)(2,1)S(1)}, u32[]{:S(2)}, u32[]{:S(2)}) async-start(bf16[8,160,256]{2,1,0:T(8,128)(2,1)} %attention.1), calls=%async_computation.1 | async-start | bytes 1310720 | tf_op jit(solution)/shard_map/all_to_all | solution.py:245
  63.9 78.0 %all-gather.6.cloned.1.call-start = ((), (), s32[]{:S(2)}) async-start(), calls=%async_computation.9 | async-start | bytes 5898240 | tf_op jit(solution)/shard_map/all_gather | solution.py:249
  108.5 146.2 %all-gather.4.cloned.1.call-start = ((), (), s32[]{:S(2)}) async-start(), calls=%async_computation.7 | async-start | bytes 10813440 | tf_op jit(solution)/shard_map/all_gather | solution.py:223
  265.9 4.9 %copy-start.6 = (s32[64]{0:T(128)S(1)}, s32[64]{0:T(128)}, u32[]{:S(2)}) copy-start(s32[64]{0:T(128)} %param.21) | copy-start | bytes 772
  265.9 19.5 %copy-start.5 = (f32[8192]{0:T(1024)S(1)}, f32[8192]{0:T(1024)}, u32[]{:S(2)}) copy-start(f32[8192]{0:T(1024)} %param.18) | copy-start | bytes 98308
  265.9 19.4 %all-to-all-start.3 = ((bf16[8,64,1024]{2,1,0:T(8,128)(2,1)}), bf16[8,64,1024]{2,1,0:T(8,128)(2,1)S(1)}, u32[]{:S(2)}, u32[]{:S(2)}) async-start(bf16[8,64,1024]{2,1,0:T(8,128)(2,1)} %project.1), calls=%async_computation.3 | async-start | bytes 2097152 | tf_op jit(solution)/shard_map/all_to_all | solution.py:262
  270.8 87.5 %reduce-scatter.2.cloned.1.call-start = ((), (), s32[]{:S(2)}) async-start(), calls=%async_computation.8 | async-start | bytes 5898240 | tf_op jit(solution)/shard_map/reduce_scatter | solution.py:286
  285.3 1.6 copy-start
  358.4 1.1 copy-start.4
  360.9 30.1 %all-to-all-start.5 = ((bf16[32,16,640]{2,1,0:T(8,128)(2,1)}), bf16[32,16,640]{2,1,0:T(8,128)(2,1)S(1)}, u32[]{:S(2)}, u32[]{:S(2)}) async-start(bf16[32,16,640]{2,1,0:T(8,128)(2,1)} %to_granules.1), calls=%async_computation.6 | async-start | bytes 1310720 | tf_op jit(solution)/shard_map/all_to_all | solution.py:288
Sparse Core Ops, SparseCore 0:
  108.6 33.2 all-gather.5
  144.5 110.0 all-gather.3
  323.4 34.9 reduce-scatter.1

commit v2 on v1

v2 whole, which is shorter than its diff:
```python
import jax
import jax.numpy as jnp
from jax import lax
from jax.experimental import pallas as pl
from jax.experimental.pallas import tpu as pltpu
from jax.sharding import PartitionSpec as P

VISION_WIDTH = 1280
HEAD_DIM = 80
MERGER_FEATURES = 5120
ROWS = 64
HALF = 640
EPS = 1e-06
NT = (((1,), (1,)), ((), ()))
F32 = jnp.float32
BF16 = jnp.bfloat16
LOG2E = 1.4426950408889634
MESH = pl.DeviceIdType.MESH
DMA = pltpu.SemaphoreType.DMA
ANY = pl.BlockSpec(memory_space=pl.ANY)
VMEM = pl.BlockSpec(memory_space=pltpu.VMEM)


def iota(shape, axis):
    return lax.broadcasted_iota(jnp.int32, shape, axis)


def eye(n):
    return (iota((n, n), 0) == iota((n, n), 1)).astype(F32).astype(BF16)


def mm(a, b):
    return jnp.dot(a, b, preferred_element_type=F32)


def mm_nt(a, b):
    return lax.dot_general(a, b, NT, preferred_element_type=F32)


def onehot(mask):
    return mask.astype(F32).astype(BF16)


def block_of_granule(rho):
    g, half, i, p = rho // 16, rho // 8 % 2, rho // 4 % 2, rho % 4
    return (p * 2 + half) * 64 + g * 2 + i


def attention(x_ref, o_ref, k_scr, idk_scr, s_scr):
    one = eye(256)
    scale = HEAD_DIM ** (-0.5) * LOG2E
    first, last, id_rows = [], [], []
    for j in range(8):
        for h in range(2):
            k_scr[j, h] = mm_nt(one, x_ref[j, 160 + 80 * h : 240 + 80 * h, :]).astype(BF16)
        parts = x_ref[j, 480:496, :]
        cols = mm_nt(one, parts)
        idk_scr[j] = jnp.broadcast_to(cols[:, 0:1] * 16.0 + cols[:, 1:2], (256, 128))
        parts = parts.astype(F32)
        row = parts[0:1] * 16.0 + parts[1:2]
        first.append(jnp.min(row))
        last.append(jnp.max(row))
    for i in range(8):
        parts = x_ref[i, 480:496, :].astype(F32)
        idq = parts[0:1] * 16.0 + parts[1:2]
        lo, hi = jnp.int32(0), jnp.int32(8)
        for j in range(8):
            if j < i:
                lo = lo + jnp.where(last[j] < first[i], 1, 0)
            if j > i:
                hi = hi - jnp.where(first[j] > last[i], 1, 0)

        def scores(j, m):
            idk = idk_scr[j]
            same = jnp.concatenate([idk, idk], axis=1) == idq
            new = []
            for h in range(2):
                s = mm(k_scr[j, h], x_ref[i, 80 * h : 80 * h + 80, :])
                s = jnp.where(same, s, -1e30)
                s_scr[h, j] = s
                new.append(jnp.maximum(m[h], jnp.max(s.reshape(32, 8, 256), axis=0)))
            return tuple(new)

        m = lax.fori_loop(lo, hi, scores, (jnp.full((8, 256), -1e30, F32),) * 2)
        top = [jnp.max(m[h], axis=0, keepdims=True) for h in range(2)]

        def weighted(j, carry):
            new = []
            for h in range(2):
                acc, total = carry[h]
                p = jnp.exp2((s_scr[h, j] - top[h]) * scale)
                total = total + jnp.sum(p.reshape(32, 8, 256), axis=0)
                acc = acc + mm(x_ref[j, 320 + 80 * h : 400 + 80 * h, :], p.astype(BF16))
                new.append((acc, total))
            return tuple(new)

        zero = (jnp.zeros((HEAD_DIM, 256), F32), jnp.zeros((8, 256), F32))
        done = lax.fori_loop(lo, hi, weighted, (zero, zero))
        for h in range(2):
            acc, total = done[h]
            total = jnp.sum(total, axis=0, keepdims=True)
            o_ref[i, 80 * h : 80 * h + 80, :] = (acc / total).astype(BF16)


def normalize(attn_t, one):
    x = jnp.concatenate([mm_nt(one, attn_t[256 * f : 256 * f + 256, :]) for f in range(5)], axis=1)
    x = x - jnp.mean(x, axis=1, keepdims=True)
    rstd = lax.rsqrt(jnp.mean(x * x, axis=1, keepdims=True) + EPS)
    return x * rstd, rstd


def greet(devices):
    barrier = pltpu.get_barrier_semaphore()
    for device in devices:
        pl.semaphore_signal(barrier, inc=1, device_id=device, device_id_type=MESH)
    pl.semaphore_wait(barrier, len(devices))


def remote(src, dst, send_sem, recv_sem, device):
    return pltpu.make_async_remote_copy(
        src_ref=src, dst_ref=dst, send_sem=send_sem, recv_sem=recv_sem, device_id=device, device_id_type=MESH
    )


def others(axis, n):
    me = lax.axis_index(axis)
    return [{axis: lax.rem(me + k, n)} for k in range(1, n)]


def exchange(axis, n, src, dst, send_sem, recv_sem, local_sem):
    me = lax.axis_index(axis)
    copies = []
    for k in range(1, n):
        d = lax.rem(me + k, n)
        copy = remote(src.at[d], dst.at[me], send_sem.at[k], recv_sem.at[k], {axis: d})
        copy.start()
        copies.append(copy)
    own = pltpu.make_async_copy(src.at[me], dst.at[me], local_sem)
    own.start()
    return copies + [own]


def finish(copies):
    for copy in copies:
        copy.wait()


def heads_out(q_ref, k_ref, v_ref, ids_ref, out_ref, parts, send_sem, recv_sem, local_sem):
    one = eye(256)
    for t, ref in enumerate((q_ref, k_ref, v_ref)):
        for f in range(5):
            block = mm_nt(one, ref[:, 256 * f : 256 * f + 256]).astype(BF16)
            lower = 256 * f
            while lower < 256 * f + 256:
                dev = lower // 160
                upper = min(160 * (dev + 1), 256 * f + 256)
                parts[dev, 160 * t + lower - 160 * dev : 160 * t + upper - 160 * dev, :] = block[
                    lower - 256 * f : upper - 256 * f, :
                ]
                lower = upper
    ids = ids_ref[...]
    rows = jnp.where(iota((16, 256), 0) % 2 == 0, ids // 16, ids % 16)
    rows = rows.astype(F32).astype(BF16)
    for dev in range(8):
        parts[dev, 480:496, :] = rows
    greet(others("seq", 8))
    finish(exchange("seq", 8, parts, out_ref, send_sem, recv_sem, local_sem))


def neighbours():
    me = lax.axis_index("seq")
    x, core = me // 2, lax.rem(me, 2)
    chip = lambda k: lax.rem(x + k, 4) * 2 + core
    return me, chip(1), chip(3), chip(2), x * 2 + 1 - core


def merge_and_gather(
    o_ref, gain_ref, target_ref, attn_ref, a_ref, granules, routed, s1, r1, s2, r2, l_sem, s3, r3
):
    greet(others("seq", 8) + others("grp", 32))
    finish(exchange("seq", 8, o_ref, attn_ref, s1, r1, l_sem))
    xhat, _ = normalize(attn_ref[...].reshape(VISION_WIDTH, 256), eye(256))
    merged = (xhat * gain_ref[...]).astype(BF16)
    stacked = jnp.concatenate([merged[:, :HALF], merged[:, HALF:]], axis=0)
    pick = onehot(iota((512, 512), 0) == target_ref[...])
    granules[...] = mm(pick, stacked).astype(BF16).reshape(32, 16, HALF)
    finish(exchange("grp", 32, granules, routed, s2, r2, l_sem))
    me, right, left, across, twin = neighbours()
    pick = onehot(iota((512, 512), 0) == block_of_granule(iota((512, 512), 1)))
    mine = mm(pick, routed[...].reshape(512, HALF)).astype(BF16)
    for b in range(8):
        a_ref[b, me] = mine[64 * b : 64 * b + 64]
    upper, lower = pl.ds(0, 32), pl.ds(32, 32)

    def piece(kind, b, owner, rows, device):
        place = a_ref.at[b, owner] if rows is None else a_ref.at[b, owner, rows]
        return remote(place, place, s3.at[kind, b], r3.at[kind, b], {"seq": device})

    def own(kind, b):
        return piece(kind, b, me, None, (right, left, twin)[kind])

    def forward(kind, b):
        if kind == 3:
            return piece(3, b, left, upper, right)
        return piece(4, b, right, lower, left)

    def to_twin(kind, b):
        owner = (left, right, across, across)[kind - 5]
        return piece(kind, b, owner, (None, None, upper, lower)[kind - 5], twin)

    def first(b, _):
        for kind in range(3):
            own(kind, b).start()
        return 0

    def second(b, _):
        own(0, b).wait_recv()
        forward(3, b).start()
        to_twin(5, b).start()
        own(1, b).wait_recv()
        forward(4, b).start()
        to_twin(6, b).start()
        return 0

    def third(b, _):
        forward(3, b).wait_recv()
        to_twin(7, b).start()
        forward(4, b).wait_recv()
        to_twin(8, b).start()
        return 0

    def last(b, _):
        own(0, b).wait_send()
        own(1, b).wait_send()
        own(2, b).wait()
        forward(3, b).wait_send()
        forward(4, b).wait_send()
        for kind in range(5, 9):
            to_twin(kind, b).wait()
        return 0

    for step in (first, second, third, last):
        lax.fori_loop(0, 8, step, 0)


def language(
    a_ref, w_ref, text_ref, cot_ref, gain_ref, pos_ref, posc_ref, attn_ref, mgain_ref, target_ref,
    hid_ref, out_ref,
    w, text, cot, proj, vis, inp_scr, back, ret, terms, twin_terms, far, near, summed, granules, arrived,
    w_sem, t_sem, s1, r1, s2, r2, s3, r3, s4, r4, l_sem,
):
    loads = [pltpu.make_async_copy(w_ref.at[:, pl.ds(256 * n, 256)], w.at[n], w_sem.at[n]) for n in range(4)]
    loads += [pltpu.make_async_copy(text_ref, text, t_sem.at[0]), pltpu.make_async_copy(cot_ref, cot, t_sem.at[1])]
    for load in loads:
        load.start()
    greet(others("seq", 8) + others("grp", 32))
    me, right, left, across, twin = neighbours()

    def vision_tile(n, k):
        d = lax.rem(me + k, 8)
        return remote(proj.at[n, d], vis.at[n, me], s1.at[n, k], r1.at[n, k], {"seq": d})

    def project(n, _):
        pltpu.make_async_copy(w_ref.at[:, pl.ds(0, 256)], w.at[n], w_sem.at[n]).wait()
        total = jnp.zeros((512, 256), F32)
        for b in range(8):
            total = total + mm(a_ref[b].reshape(512, HALF), w[n, HALF * b : HALF * b + HALF, :])
        proj[n] = total.astype(BF16).reshape(8, ROWS, 256)
        for k in range(1, 8):
            vision_tile(n, k).start()
        vis[n, me] = proj[n, me]
        return 0

    lax.fori_loop(0, 4, project, 0)
    loads[4].wait()
    loads[5].wait()

    place = onehot(iota((128, ROWS), 0) == pos_ref[...])
    pick = onehot(iota((ROWS, 128), 1) == posc_ref[...])
    taken = jnp.sum(place.astype(F32), axis=1, keepdims=True) > 0.5

    def place_tile(n, carry):
        for k in range(1, 8):
            vision_tile(n, k).wait_recv()

        def block(c, carry):
            squares, products = carry
            cols = pl.ds(pl.multiple_of(c * 1024 + n * 256, 256), 256)
            inp = jnp.where(taken, mm(place, vis[n, c]), text[:, cols].astype(F32))
            inp_scr[:, cols] = inp
            gy = cot[:, cols].astype(F32) * gain_ref[:, cols]
            return squares + inp * inp, products + gy * inp

        return lax.fori_loop(0, 8, block, carry)

    zero = jnp.zeros((128, 256), F32)
    squares, products = lax.fori_loop(0, 4, place_tile, (zero, zero))
    squares = jnp.sum(squares, axis=1, keepdims=True)
    products = jnp.sum(products, axis=1, keepdims=True)
    r = lax.rsqrt(squares / 8192.0 + EPS)
    slope = r * r * (products / 8192.0)

    def back_copy(k):
        d = lax.rem(me + k, 8)
        return remote(back.at[d], ret.at[me], s2.at[k], r2.at[k], {"seq": d})

    def grads(k, _):
        c = lax.rem(me + k, 8)
        cols = pl.ds(pl.multiple_of(c * 1024, 1024), 1024)
        gy = cot[:, cols].astype(F32) * gain_ref[:, cols]
        grad = (r * (gy - inp_scr[:, cols] * slope)).astype(BF16)
        back[c] = mm(pick, grad).astype(BF16)
        back_copy(k).start()
        return 0

    lax.fori_loop(1, 8, grads, 0)
    cols = pl.ds(pl.multiple_of(me * 1024, 1024), 1024)
    gy = cot[:, cols].astype(F32) * gain_ref[:, cols]
    grad = (r * (gy - inp_scr[:, cols] * slope)).astype(BF16)
    ret[me] = mm(pick, grad).astype(BF16)

    def hidden(c, _):
        cols = pl.ds(pl.multiple_of(c * 1024, 1024), 1024)
        hid_ref[:, cols] = (inp_scr[:, cols] * r * gain_ref[:, cols]).astype(BF16)
        return 0

    lax.fori_loop(0, 8, hidden, 0)
    for k in range(1, 8):
        back_copy(k).wait_recv()

    core = lax.rem(me, 2)
    x = me // 2
    chip_right, chip_left, chip_across = lax.rem(x + 1, 4), lax.rem(x + 3, 4), lax.rem(x + 2, 4)
    upper, lower = pl.ds(0, 32), pl.ds(32, 32)

    def to_twin(b):
        return remote(terms.at[b, 1 - core], twin_terms.at[b], s3.at[0, b], r3.at[0, b], {"seq": twin})

    def far_right(b):
        return remote(terms.at[b, core, chip_across, upper], far.at[b, upper], s3.at[1, b], r3.at[1, b], {"seq": right})

    def far_left(b):
        return remote(terms.at[b, core, chip_across, lower], far.at[b, lower], s3.at[2, b], r3.at[2, b], {"seq": left})

    def near_right(b):
        return remote(terms.at[b, core, chip_right], near.at[b, 0], s3.at[3, b], r3.at[3, b], {"seq": right})

    def near_left(b):
        return remote(terms.at[b, core, chip_left], near.at[b, 1], s3.at[4, b], r3.at[4, b], {"seq": left})

    def step(i, _):
        @pl.when(i < 8)
        def _():
            b = i
            rows = pl.ds(pl.multiple_of(b * HALF, HALF), HALF)
            total = jnp.zeros((512, HALF), F32)
            for n in range(4):
                total = total + mm_nt(ret[:, :, 256 * n : 256 * n + 256].reshape(512, 256), w[n, rows, :])
            total = total.astype(BF16)
            for s in range(8):
                terms[b, s % 2, s // 2] = total[64 * s : 64 * s + 64]
            to_twin(b).start()

        @pl.when((i >= 1) & (i < 9))
        def _():
            b = i - 1
            to_twin(b).wait_recv()
            both = terms[b, core].astype(F32) + twin_terms[b].astype(F32)
            terms[b, core] = both.astype(BF16)
            far_right(b).start()
            far_left(b).start()

        @pl.when((i >= 2) & (i < 10))
        def _():
            b = i - 2
            far_right(b).wait_recv()
            terms[b, core, chip_right, upper] = (
                terms[b, core, chip_right, upper].astype(F32) + far[b, upper].astype(F32)
            ).astype(BF16)
            near_right(b).start()
            far_left(b).wait_recv()
            terms[b, core, chip_left, lower] = (
                terms[b, core, chip_left, lower].astype(F32) + far[b, lower].astype(F32)
            ).astype(BF16)
            near_left(b).start()

        @pl.when(i >= 3)
        def _():
            b = i - 3
            near_right(b).wait_recv()
            near_left(b).wait_recv()
            total = terms[b, core, x].astype(F32) + near[b, 0].astype(F32) + near[b, 1].astype(F32)
            summed[b] = total.astype(BF16)

        return 0

    lax.fori_loop(0, 11, step, 0)
    pick = onehot(block_of_granule(iota((512, 512), 0)) == iota((512, 512), 1))
    granules[...] = mm(pick, summed[...].reshape(512, HALF)).astype(BF16).reshape(32, 16, HALF)
    copies = exchange("grp", 32, granules, arrived, s4, r4, l_sem)

    def settle(b, _):
        for copy in (to_twin(b), far_right(b), far_left(b), near_right(b), near_left(b)):
            copy.wait_send()
        return 0

    lax.fori_loop(0, 8, settle, 0)
    for n in range(4):
        for k in range(1, 8):
            vision_tile(n, k).wait_send()
    for k in range(1, 8):
        back_copy(k).wait_send()
    xhat, rstd = normalize(attn_ref[...].reshape(VISION_WIDTH, 256), eye(256))
    pick = onehot(iota((512, 512), 1) == target_ref[...])
    finish(copies)
    grads = mm(pick, arrived[...].reshape(512, HALF))
    gy = jnp.concatenate([grads[:256], grads[256:]], axis=1) * mgain_ref[...]
    mean = jnp.mean(gy, axis=1, keepdims=True)
    along = jnp.mean(gy * xhat, axis=1, keepdims=True)
    out_ref[...] = (rstd * (gy - mean - xhat * along)).astype(BF16)


def params(collective_id=None):
    if collective_id is None:
        return pltpu.CompilerParams(vmem_limit_bytes=48 * 2**20)
    return pltpu.CompilerParams(
        vmem_limit_bytes=58 * 2**20, collective_id=collective_id, has_side_effects=True
    )


def shaped(*shape, dtype=BF16):
    return jax.ShapeDtypeStruct(shape, dtype)


def body(
    queries,
    key_rows,
    values,
    segment_ids,
    merger_norm_gain,
    merge_weight,
    text_rows,
    token_gain,
    cotangent,
    send_slot,
    place_pos,
):
    w = lax.all_gather(merge_weight, "grp", axis=0, tiled=True)
    gain = merger_norm_gain.reshape(1, VISION_WIDTH)
    slot = jnp.tile(jnp.repeat(send_slot, 4), 2)
    kappa = jnp.arange(512, dtype=jnp.int32)
    target = slot // 2 * 16 + kappa // 256 * 8 + slot % 2 * 4 + kappa % 4

    x = pl.pallas_call(
        heads_out,
        out_shape=shaped(8, 496, 256),
        in_specs=[VMEM] * 4,
        out_specs=VMEM,
        scratch_shapes=[pltpu.VMEM((8, 496, 256), BF16), DMA((8,)), DMA((8,)), DMA(())],
        compiler_params=params(1),
        name="heads_out",
    )(queries, key_rows, values, segment_ids.reshape(1, 256))
    o = pl.pallas_call(
        attention,
        out_shape=shaped(8, 160, 256),
        in_specs=[VMEM],
        out_specs=VMEM,
        scratch_shapes=[
            pltpu.VMEM((8, 2, 256, HEAD_DIM), BF16),
            pltpu.VMEM((8, 256, 128), F32),
            pltpu.VMEM((2, 8, 256, 256), F32),
        ],
        compiler_params=params(),
        name="attention",
    )(x)
    attn, a = pl.pallas_call(
        merge_and_gather,
        out_shape=[shaped(8, 160, 256), shaped(8, 8, ROWS, HALF)],
        in_specs=[VMEM] * 3,
        out_specs=[VMEM] * 2,
        scratch_shapes=[
            pltpu.VMEM((32, 16, HALF), BF16),
            pltpu.VMEM((32, 16, HALF), BF16),
            DMA((8,)),
            DMA((8,)),
            DMA((32,)),
            DMA((32,)),
            DMA(()),
            DMA((9, 8)),
            DMA((9, 8)),
        ],
        compiler_params=params(2),
        name="merge_and_gather",
    )(o, gain, target.reshape(1, 512))
    return pl.pallas_call(
        language,
        out_shape=[shaped(128, 8192), shaped(256, VISION_WIDTH)],
        in_specs=[VMEM, ANY, ANY, ANY] + [VMEM] * 6,
        out_specs=[VMEM] * 2,
        scratch_shapes=[
            pltpu.VMEM((4, MERGER_FEATURES, 256), BF16),
            pltpu.VMEM((128, 8192), BF16),
            pltpu.VMEM((128, 8192), BF16),
            pltpu.VMEM((4, 8, ROWS, 256), BF16),
            pltpu.VMEM((4, 8, ROWS, 256), BF16),
            pltpu.VMEM((128, 8192), F32),
            pltpu.VMEM((8, ROWS, 1024), BF16),
            pltpu.VMEM((8, ROWS, 1024), BF16),
            pltpu.VMEM((8, 2, 4, ROWS, HALF), BF16),
            pltpu.VMEM((8, 4, ROWS, HALF), BF16),
            pltpu.VMEM((8, ROWS, HALF), BF16),
            pltpu.VMEM((8, 2, ROWS, HALF), BF16),
            pltpu.VMEM((8, ROWS, HALF), BF16),
            pltpu.VMEM((32, 16, HALF), BF16),
            pltpu.VMEM((32, 16, HALF), BF16),
            DMA((4,)),
            DMA((2,)),
            DMA((4, 8)),
            DMA((4, 8)),
            DMA((8,)),
            DMA((8,)),
            DMA((5, 8)),
            DMA((5, 8)),
            DMA((32,)),
            DMA((32,)),
            DMA(()),
        ],
        compiler_params=params(3),
        name="language",
    )(
        a,
        w,
        text_rows,
        cotangent,
        token_gain.reshape(1, 8192),
        place_pos.reshape(1, ROWS),
        place_pos.reshape(ROWS, 1),
        attn,
        gain,
        target.reshape(512, 1),
    )


def solution(mesh):
    in_specs = (
        P(("grp", "seq"), None),
        P(("grp", "seq"), None),
        P(("grp", "seq"), None),
        P(("grp", "seq")),
        P(),
        P("grp", "seq"),
        P(("grp", "seq"), None),
        P(),
        P(("grp", "seq"), None),
        P(("grp", "seq")),
        P(("grp", "seq")),
    )
    out_specs = (P(("grp", "seq"), None), P(("grp", "seq"), None))
    return jax.shard_map(body, mesh=mesh, in_specs=in_specs, out_specs=out_specs, check_vma=False)
```

time: 402 us -> 243 us (0.60)
  waiting for transfers between devices: 225 us -> 0.68 us
  Pallas kernels: 52.9 us -> 216 us
  blocking collectives: 80.1 us -> 0 us
  starting transfers between devices: 19.8 us -> 0.04 us
    pallas_call x9 -> x4, Pallas kernels: 52.9 us -> 216 us  [the longest x1 89.2 us: body(): pl.pallas_call(language, out_shape=[shaped(128, 8192), shaped(256, VISION...]
    all_gather x1, waiting for transfers between devices: 113 us -> 0.01 us  [body(): w = lax.all_gather(merge_weight, 'grp', axis=0, tiled=True)]
    all_to_all x3 -> x0, blocking collectives: 80.1 us -> none  [the longest x1 31.6 us: body(): lax.all_to_all(routed, 'grp', split_axis=0, concat_axis=0, tiled=True)]
    all_to_all x3 -> x0, waiting for transfers between devices: 44.2 us -> none  [the longest x1 19.8 us: body(): lax.all_to_all(granules, 'grp', split_axis=0, concat_axis=0, tiled=True)]
    reduce_scatter x1 -> x0, waiting for transfers between devices: 35.1 us -> none  [body(): lax.psum_scatter(terms.reshape(8 * 512, HALF), 'seq', scatter_dimension=0...]
    all_gather x1 -> x0, waiting for transfers between devices: 32.7 us -> none  [body(): gathered = lax.all_gather(blocks, 'seq', axis=0)]
    all_to_all x3 -> x0, starting transfers between devices: 19.7 us -> none  [the longest x1 9.85 us: body(): lax.all_to_all(granules, 'grp', split_axis=0, concat_axis=0, tiled=True)]
  transfers between devices with their start and end apart: 6 -> 1, of which waited for: 6 -> 0; matrix products, arithmetic and copies ran while one was open for 0% -> 2% of each run, Pallas kernels for 0% -> 52%
where the time goes in v2:
time: 243 us
  Pallas kernels  216 us (89%)
  between operations  14.1 us (6%)
  local copies, waits for them, and re-layouts  10.1 us (4%)
    pallas_call x1, Pallas kernels, body(): pl.pallas_call(language, out_shape=[shaped(128, 8192), shaped(256, VISION...  89.2 us
    pallas_call x1, Pallas kernels, body(): pl.pallas_call(merge_and_gather, out_shape=[shaped(8, 160, 256), shaped(8...  81.5 us
    pallas_call x1, Pallas kernels, body(): pl.pallas_call(heads_out, out_shape=shaped(8, 496, 256), in_specs=[VMEM]...  28.4 us
    pallas_call x1, Pallas kernels, body(): pl.pallas_call(attention, out_shape=shaped(8, 160, 256), in_specs=[VMEM],...  17.2 us
    unnamed x11, local copies, waits for them, and re-layouts  6.57 us
  transfers between devices with their start and end apart: 1, of which 0 were waited for; matrix products, arithmetic and copies ran while one was open for 2% of the time, Pallas kernels for 52%

profile of v2, /device:TPU:2, one launch (start us, length us, event | category | flops | bytes accessed | tf_op | source)
XLA Modules:
  0.0 242.8 jit_solution(6360916040672039078)
XLA Ops:
  7.2 0.0 all-gather.2.cloned.1.call-start
  7.2 0.7 all-gather.2.cloned.1.call-update
  7.9 1.3 reshape.359.gain_ref.mgain_ref
  9.2 0.7 broadcast_in_dim.3
  9.9 0.1 tile.12
  10.0 1.4 copy.24.posc_ref
  11.4 0.1 copy.27
  11.6 28.4 %heads_out.1.x_ref = bf16[8,496,256]{2,1,0:T(8,128)(2,1)} custom-call(bf16[256,1280]{1,0:T(8,128)(2,1)} %q_ref.1, bf16[256,1280]{1,0:T(8,128)(2,1)} %k_ref.1, bf16[256,1280]{1,0:T(8,128)(2,1)} %v_ref.1, s32[1,256]{1,0:T(1,128)} %bitcast.36), custom_call_target="tpu_custom_call" | custom-call | tf_op jit(solution)/shard_map/heads_out/pallas_call | solution.py:454
  40.0 0.0 copy-start
  40.0 1.6 copy-done
  41.6 17.2 %attention.1.o_ref = bf16[8,160,256]{2,1,0:T(8,128)(2,1)S(1)} custom-call(bf16[8,496,256]{2,1,0:T(8,128)(2,1)S(1)} %copy-done), custom_call_target="tpu_custom_call" | custom-call | tf_op jit(solution)/shard_map/attention/pallas_call | solution.py:463
  58.7 0.0 copy-start.1
  58.8 0.8 copy-done.1
  59.6 0.6 fusion.17.target_ref
  60.2 81.5 %merge_and_gather.1 = (bf16[8,160,256]{2,1,0:T(8,128)(2,1)}, bf16[8,8,64,640]{3,2,1,0:T(8,128)(2,1)}) custom-call(bf16[8,160,256]{2,1,0:T(8,128)(2,1)} %copy-done.1, f32[1,1280]{1,0:T(1,128)} %reshape.359.gain_ref.mgain_ref, s32[1,512]{1,0:T(1,128)} %fusion.17.target_ref), custom_call_target="tpu_custom_call" | custom-call | tf_op jit(solution)/shard_map/merge_and_gather/pallas_call | solution.py:476
  141.7 1.0 fusion.3.target_ref
  142.7 0.0 all-gather.2.cloned.1.call-done.w_ref
  142.7 89.2 %language.1 = (bf16[128,8192]{1,0:T(8,128)(2,1)}, bf16[256,1280]{1,0:T(8,128)(2,1)}) custom-call(bf16[8,8,64,640]{3,2,1,0:T(8,128)(2,1)} %get-tuple-element.4.a_ref, bf16[5120,1024]{1,0:T(8,128)(2,1)} %all-gather.2.cloned.1.call-done.w_ref, bf16[128,8192]{1,0:T(8,128)(2,1)} %text_ref.1, bf16[128,8192]{1,0:T(8,128)(2,1)} %cot_ref.1, f32[1,8192]{1,0:T(1,128)} %bitcast.31, ...), custom_call_target="tpu_custom_call" | custom-call | tf_op jit(solution)/shard_map/language/pallas_call | solution.py:495
  231.9 0.0 copy-start.2
  232.0 3.2 %copy.30 = bf16[128,8192]{1,0:T(8,128)(2,1)} copy(bf16[128,8192]{1,0:T(8,128)(2,1)} %get-tuple-element.8) | data formatting | bytes 4194304
  235.1 0.0 copy-done.2
  235.1 0.8 copy.31
  (2 shorter events, 0.0 us)
Async XLA Ops:
  7.2 135.5 %all-gather.2.cloned.1.call-start = ((), (), s32[]{:S(2)}) async-start(), calls=%async_computation | async-start | bytes 10813440 | tf_op jit(solution)/shard_map/all_gather | solution.py:448
  40.0 1.6 copy-start
  58.7 0.8 copy-start.1
  231.9 3.2 %copy-start.2 = (bf16[256,1280]{1,0:T(8,128)(2,1)S(1)}, bf16[256,1280]{1,0:T(8,128)(2,1)}, u32[]{:S(2)}) copy-start(bf16[256,1280]{1,0:T(8,128)(2,1)} %get-tuple-element.9) | copy-start | bytes 1966084
Sparse Core Ops, SparseCore 0:
  10.6 126.1 all-gather.1

commit v3 on v2

v3 whole, which is shorter than its diff:
```python
import jax
import jax.numpy as jnp
from jax import lax
from jax.experimental import pallas as pl
from jax.experimental.pallas import tpu as pltpu
from jax.sharding import PartitionSpec as P

VISION_WIDTH = 1280
HEAD_DIM = 80
MERGER_FEATURES = 5120
ROWS = 64
PART = 32
HALF = 640
EPS = 1e-06
NT = (((1,), (1,)), ((), ()))
F32 = jnp.float32
BF16 = jnp.bfloat16
LOG2E = 1.4426950408889634
MESH = pl.DeviceIdType.MESH
DMA = pltpu.SemaphoreType.DMA
ANY = pl.BlockSpec(memory_space=pl.ANY)
VMEM = pl.BlockSpec(memory_space=pltpu.VMEM)


def iota(shape, axis):
    return lax.broadcasted_iota(jnp.int32, shape, axis)


def eye(n):
    return (iota((n, n), 0) == iota((n, n), 1)).astype(F32).astype(BF16)


def mm(a, b):
    return jnp.dot(a, b, preferred_element_type=F32)


def mm_nt(a, b):
    return lax.dot_general(a, b, NT, preferred_element_type=F32)


def onehot(mask):
    return mask.astype(F32).astype(BF16)


def block_of_granule(rho):
    kk, half, i, p = rho // 16, rho // 8 % 2, rho // 4 % 2, rho % 4
    return (p * 2 + half) * PART + kk * 2 + i


def attention(x_ref, o_ref, k_scr, idk_scr, s_scr):
    one = eye(256)
    scale = HEAD_DIM ** (-0.5) * LOG2E
    first, last, id_rows = [], [], []
    for j in range(8):
        for h in range(2):
            k_scr[j, h] = mm_nt(one, x_ref[j, 160 + 80 * h : 240 + 80 * h, :]).astype(BF16)
        parts = x_ref[j, 480:496, :]
        cols = mm_nt(one, parts)
        idk_scr[j] = jnp.broadcast_to(cols[:, 0:1] * 16.0 + cols[:, 1:2], (256, 128))
        parts = parts.astype(F32)
        row = parts[0:1] * 16.0 + parts[1:2]
        first.append(jnp.min(row))
        last.append(jnp.max(row))
    for i in range(8):
        parts = x_ref[i, 480:496, :].astype(F32)
        idq = parts[0:1] * 16.0 + parts[1:2]
        lo, hi = jnp.int32(0), jnp.int32(8)
        for j in range(8):
            if j < i:
                lo = lo + jnp.where(last[j] < first[i], 1, 0)
            if j > i:
                hi = hi - jnp.where(first[j] > last[i], 1, 0)

        def scores(j, m):
            idk = idk_scr[j]
            same = jnp.concatenate([idk, idk], axis=1) == idq
            new = []
            for h in range(2):
                s = mm(k_scr[j, h], x_ref[i, 80 * h : 80 * h + 80, :])
                s = jnp.where(same, s, -1e30)
                s_scr[h, j] = s
                new.append(jnp.maximum(m[h], jnp.max(s.reshape(32, 8, 256), axis=0)))
            return tuple(new)

        m = lax.fori_loop(lo, hi, scores, (jnp.full((8, 256), -1e30, F32),) * 2)
        top = [jnp.max(m[h], axis=0, keepdims=True) for h in range(2)]

        def weighted(j, carry):
            new = []
            for h in range(2):
                acc, total = carry[h]
                p = jnp.exp2((s_scr[h, j] - top[h]) * scale)
                total = total + jnp.sum(p.reshape(32, 8, 256), axis=0)
                acc = acc + mm(x_ref[j, 320 + 80 * h : 400 + 80 * h, :], p.astype(BF16))
                new.append((acc, total))
            return tuple(new)

        zero = (jnp.zeros((HEAD_DIM, 256), F32), jnp.zeros((8, 256), F32))
        done = lax.fori_loop(lo, hi, weighted, (zero, zero))
        for h in range(2):
            acc, total = done[h]
            total = jnp.sum(total, axis=0, keepdims=True)
            o_ref[i, 80 * h : 80 * h + 80, :] = (acc / total).astype(BF16)


def normalize(attn_t, one):
    x = jnp.concatenate([mm_nt(one, attn_t[256 * f : 256 * f + 256, :]) for f in range(5)], axis=1)
    x = x - jnp.mean(x, axis=1, keepdims=True)
    rstd = lax.rsqrt(jnp.mean(x * x, axis=1, keepdims=True) + EPS)
    return x * rstd, rstd


def greet(devices):
    barrier = pltpu.get_barrier_semaphore()
    for device in devices:
        pl.semaphore_signal(barrier, inc=1, device_id=device, device_id_type=MESH)
    pl.semaphore_wait(barrier, len(devices))


def remote(src, dst, send_sem, recv_sem, device):
    return pltpu.make_async_remote_copy(
        src_ref=src, dst_ref=dst, send_sem=send_sem, recv_sem=recv_sem, device_id=device, device_id_type=MESH
    )


def others(axis, n):
    me = lax.axis_index(axis)
    return [{axis: lax.rem(me + k, n)} for k in range(1, n)]


def exchange(src, dst, send_sem, recv_sem, local_sem):
    me = lax.axis_index("seq")
    copies = []
    for k in range(1, 8):
        d = lax.rem(me + k, 8)
        copy = remote(src.at[d], dst.at[me], send_sem.at[k], recv_sem.at[k], {"seq": d})
        copy.start()
        copies.append(copy)
    own = pltpu.make_async_copy(src.at[me], dst.at[me], local_sem)
    own.start()
    return copies + [own]


def finish(copies):
    for copy in copies:
        copy.wait()


def heads_out(
    q_ref, k_ref, v_ref, ids_ref, out_ref, parts, send_sem, recv_sem, local_sem
):
    one = eye(256)
    greet(others("seq", 8))
    ids = ids_ref[...]
    rows = jnp.where(iota((16, 256), 0) % 2 == 0, ids // 16, ids % 16)
    rows = rows.astype(F32).astype(BF16)
    for dev in range(8):
        parts[dev, 480:496, :] = rows
    for t, ref in enumerate((q_ref, k_ref, v_ref)):
        for f in range(5):
            block = mm_nt(one, ref[:, 256 * f : 256 * f + 256]).astype(BF16)
            lower = 256 * f
            while lower < 256 * f + 256:
                dev = lower // 160
                upper = min(160 * (dev + 1), 256 * f + 256)
                parts[dev, 160 * t + lower - 160 * dev : 160 * t + upper - 160 * dev, :] = block[
                    lower - 256 * f : upper - 256 * f, :
                ]
                lower = upper
    finish(exchange(parts, out_ref, send_sem, recv_sem, local_sem))


def neighbours():
    me = lax.axis_index("seq")
    x, core = me // 2, lax.rem(me, 2)
    chip = lambda k: lax.rem(x + k, 4) * 2 + core
    return me, chip(1), chip(3), chip(2), x * 2 + 1 - core


def granule_of_patch(slot_ref):
    slot = jnp.broadcast_to(slot_ref[...], (8, ROWS)).astype(F32).astype(BF16)
    repeat = onehot(iota((ROWS, 512), 0) == iota((ROWS, 512), 1) % 256 // 4)
    slot = mm(slot, repeat)[0:1].astype(jnp.int32)
    kappa = iota((1, 512), 1)
    target = slot // 2 * 16 + kappa // 256 * 8 + slot % 2 * 4 + kappa % 4
    return onehot(iota((512, 512), 0) == target)


def merge_and_gather(
    o_ref, gain_ref, slot_ref, attn_ref, a_ref, granules, routed, s1, r1, s2, r2, l_sem, s3, r3
):
    greet(others("seq", 8) + others("grp", 32))
    copies = exchange(o_ref, attn_ref, s1, r1, l_sem)
    g = lax.axis_index("grp")
    move = granule_of_patch(slot_ref)
    to_block = onehot(iota((256, 256), 0) == block_of_granule(iota((256, 256), 1)))
    finish(copies)
    xhat, _ = normalize(attn_ref[...].reshape(VISION_WIDTH, 256), eye(256))
    merged = (xhat * gain_ref[...]).astype(BF16)
    stacked = jnp.concatenate([merged[:, :HALF], merged[:, HALF:]], axis=0)
    granules[...] = mm(move, stacked).astype(BF16).reshape(32, 16, HALF)

    own = pltpu.make_async_copy(granules.at[g], routed.at[0, 0], l_sem)
    own.start()
    routes = [{}, {}]
    for q in range(2):
        for kk in range(1 - q, 16):
            d = lax.rem(g + 2 * kk + q, 32)
            routes[q][kk] = remote(granules.at[d], routed.at[q, kk], s2.at[q, kk], r2.at[q, kk], {"grp": d})
            routes[q][kk].start()
    me, right, left, across, twin = neighbours()
    upper, lower, both = pl.ds(0, 16), pl.ds(16, 16), pl.ds(0, 32)

    def piece(kind, q, c, owner, rows, device):
        place = a_ref.at[q, owner, rows, pl.ds(2560 * c, 2560)]
        return remote(place, place, s3.at[kind, q, c], r3.at[kind, q, c], {"seq": device})

    def gather(kind, q, c):
        if kind < 3:
            return piece(kind, q, c, me, both, (right, left, twin)[kind])
        if kind == 3:
            return piece(3, q, c, left, upper, right)
        if kind == 4:
            return piece(4, q, c, right, lower, left)
        owner = (left, right, across, across)[kind - 5]
        return piece(kind, q, c, owner, (both, both, upper, lower)[kind - 5], twin)

    def first(q):
        for copy in routes[q].values():
            copy.wait_recv()
        if q == 0:
            own.wait()
        mine = mm(to_block, routed[q].reshape(256, HALF)).astype(BF16)
        for b in range(8):
            a_ref[q, me, :, HALF * b : HALF * b + HALF] = mine[PART * b : PART * b + PART]
        for c in range(2):
            for kind in range(3):
                gather(kind, q, c).start()

    def second(q):
        for c in range(2):
            for kind in range(2):
                gather(kind, q, c).wait_recv()
                gather(3 + kind, q, c).start()
                gather(5 + kind, q, c).start()

    def third(q):
        for c in range(2):
            for kind in range(2):
                gather(3 + kind, q, c).wait_recv()
                gather(7 + kind, q, c).start()

    first(0)
    second(0)
    first(1)
    third(0)
    second(1)
    third(1)
    for q in range(2):
        for copy in routes[q].values():
            copy.wait_send()
        for c in range(2):
            for kind in range(9):
                gather(kind, q, c).wait_send()
            for kind in (2, 5, 6, 7, 8):
                gather(kind, q, c).wait_recv()


def language(
    a_ref, w_ref, text_ref, cot_ref, gain_ref, pos_ref, attn_ref, mgain_ref, slot_ref,
    hid_ref, out_ref,
    w, text, cot, picked, proj, vis, back, ret, terms, twin_terms, far, near, summed, granules, arrived,
    w_sem, t_sem, s1, r1, s2, r2, s3, r3, s4, r4, l_sem,
):
    loads = [pltpu.make_async_copy(cot_ref, cot, t_sem.at[0])]
    for n in range(2):
        rows = pl.ds(2560 * n, 2560)
        loads.append(pltpu.make_async_copy(w_ref.at[rows], w.at[rows], w_sem.at[n]))
    loads.append(pltpu.make_async_copy(text_ref, text, t_sem.at[1]))
    for load in loads:
        load.start()
    greet(others("seq", 8) + others("grp", 32))
    me, right, left, across, twin = neighbours()
    g = lax.axis_index("grp")

    place = onehot(iota((128, ROWS), 0) == pos_ref[...])
    j = iota((ROWS, ROWS), 1)
    turned = lax.rem(g + 32 - (j % PART // 2 * 2 + j // PART), 32) * 2 + j % 2
    place = mm(place, onehot(iota((ROWS, ROWS), 0) == turned)).astype(BF16)
    pick = mm_nt(eye(ROWS), place).astype(BF16)
    taken = jnp.sum(place.astype(F32), axis=1, keepdims=True) > 0.5
    loads[0].wait()
    for c in range(8):
        picked[c] = mm(pick, cot[:, 1024 * c : 1024 * c + 1024]).astype(BF16)
    for load in loads[1:]:
        load.wait()

    def vision_part(q, k):
        d = lax.rem(me + k, 8)
        return remote(proj.at[q, d], vis.at[q, me], s1.at[q, k], r1.at[q, k], {"seq": d})

    def project(q, _):
        rows = a_ref[q].reshape(256, MERGER_FEATURES)
        for n in range(4):
            cols = slice(256 * n, 256 * n + 256)
            proj[q, :, :, cols] = mm(rows, w[:, cols]).astype(BF16).reshape(8, PART, 256)
        for k in range(1, 8):
            vision_part(q, k).start()
        vis[q, me] = proj[q, me]
        return 0

    lax.fori_loop(0, 2, project, 0)

    def back_part(q, k):
        d = lax.rem(me + k, 8)
        return remote(back.at[q, d], ret.at[q, me], s2.at[q, k], r2.at[q, k], {"seq": d})

    def gains(c):
        return gain_ref[:, pl.ds(pl.multiple_of(c * 1024, 1024), 1024)]

    scales = []
    for q in range(2):
        rows = slice(PART * q, PART * q + PART)
        for k in range(1, 8):
            vision_part(q, k).wait_recv()

        def sums(c, carry):
            v = vis[q, c].astype(F32)
            gy = picked[c, rows].astype(F32) * gains(c)
            return carry[0] + v * v, carry[1] + gy * v

        zero = jnp.zeros((PART, 1024), F32)
        squares, products = lax.fori_loop(0, 8, sums, (zero, zero))
        r = lax.rsqrt(jnp.sum(squares, axis=1, keepdims=True) / 8192.0 + EPS)
        slope = r * r * (jnp.sum(products, axis=1, keepdims=True) / 8192.0)
        scales.append(r)

        def grads(c):
            gy = picked[c, rows].astype(F32) * gains(c)
            return (r * (gy - vis[q, c].astype(F32) * slope)).astype(BF16)

        def send(k, _):
            d = lax.rem(me + k, 8)
            back[q, d] = grads(d)
            back_part(q, k).start()
            return 0

        lax.fori_loop(1, 8, send, 0)
        ret[q, me] = grads(me)

    def text_squares(c, carry):
        t = text[:, pl.ds(pl.multiple_of(c * 1024, 1024), 1024)].astype(F32)
        return carry + jnp.sum(t * t, axis=1, keepdims=True)

    r_text = lax.rsqrt(lax.fori_loop(0, 8, text_squares, jnp.zeros((128, 1), F32)) / 8192.0 + EPS)

    def hidden(c, _):
        cols = pl.ds(pl.multiple_of(c * 1024, 1024), 1024)
        gain = gains(c)
        rows = jnp.concatenate([vis[q, c].astype(F32) * scales[q] for q in range(2)], axis=0) * gain
        rows = mm(place, rows.astype(BF16))
        hid_ref[:, cols] = jnp.where(taken, rows, text[:, cols].astype(F32) * r_text * gain).astype(BF16)
        return 0

    lax.fori_loop(0, 8, hidden, 0)

    core = lax.rem(me, 2)
    x = me // 2
    chip_right, chip_left, chip_across = lax.rem(x + 1, 4), lax.rem(x + 3, 4), lax.rem(x + 2, 4)
    upper, lower = pl.ds(0, 16), pl.ds(16, 16)
    halves = pl.ds(0, 2)

    def to_twin(u):
        return remote(terms.at[u, 1 - core], twin_terms.at[u], s3.at[0, u], r3.at[0, u], {"seq": twin})

    def far_right(u):
        return remote(
            terms.at[u, core, chip_across, halves, upper], far.at[u, halves, upper],
            s3.at[1, u], r3.at[1, u], {"seq": right},
        )

    def far_left(u):
        return remote(
            terms.at[u, core, chip_across, halves, lower], far.at[u, halves, lower],
            s3.at[2, u], r3.at[2, u], {"seq": left},
        )

    def near_right(u):
        return remote(terms.at[u, core, chip_right], near.at[u, 0], s3.at[3, u], r3.at[3, u], {"seq": right})

    def near_left(u):
        return remote(terms.at[u, core, chip_left], near.at[u, 1], s3.at[4, u], r3.at[4, u], {"seq": left})

    to_granule = onehot(block_of_granule(iota((256, 256), 0)) == iota((256, 256), 1))

    def route_back(q, kk):
        d = lax.rem(g + 32 - (2 * kk + q), 32)
        return remote(granules.at[q, kk], arrived.at[g], s4.at[q, kk], r4.at[q, kk], {"grp": d})

    def send_back(q):
        rows = mm(to_granule, summed[q].reshape(256, HALF)).astype(BF16)
        granules[q] = rows.reshape(16, 16, HALF)
        if q == 0:
            arrived[g] = granules[0, 0]
        for kk in range(1 - q, 16):
            route_back(q, kk).start()

    def step(i, _):
        for q in range(2):
            @pl.when(i == 4 * q)
            def _():
                for k in range(1, 8):
                    back_part(q, k).wait_recv()

        @pl.when(i < 8)
        def _():
            u = i
            rows = pl.ds(pl.multiple_of(lax.rem(u, 4) * 1280, 1280), 1280)
            total = mm_nt(ret[u // 4].reshape(256, 1024), w[rows, :]).astype(BF16)
            for s in range(8):
                for b in range(2):
                    terms[u, s % 2, s // 2, b] = total[PART * s : PART * s + PART, HALF * b : HALF * b + HALF]
            to_twin(u).start()

        @pl.when((i >= 1) & (i < 9))
        def _():
            u = i - 1
            to_twin(u).wait_recv()
            terms[u, core] = (terms[u, core].astype(F32) + twin_terms[u].astype(F32)).astype(BF16)
            far_right(u).start()
            far_left(u).start()

        @pl.when((i >= 2) & (i < 10))
        def _():
            u = i - 2
            far_right(u).wait_recv()
            terms[u, core, chip_right, :, upper] = (
                terms[u, core, chip_right, :, upper].astype(F32) + far[u, :, upper].astype(F32)
            ).astype(BF16)
            near_right(u).start()
            far_left(u).wait_recv()
            terms[u, core, chip_left, :, lower] = (
                terms[u, core, chip_left, :, lower].astype(F32) + far[u, :, lower].astype(F32)
            ).astype(BF16)
            near_left(u).start()

        @pl.when(i >= 3)
        def _():
            u = i - 3
            near_right(u).wait_recv()
            near_left(u).wait_recv()
            total = terms[u, core, x].astype(F32) + near[u, 0].astype(F32) + near[u, 1].astype(F32)
            summed[u // 4, lax.rem(u, 4)] = total.astype(BF16)

        @pl.when(i == 6)
        def _():
            send_back(0)

        return 0

    lax.fori_loop(0, 11, step, 0)
    send_back(1)

    def settle(u, _):
        for copy in (to_twin(u), far_right(u), far_left(u), near_right(u), near_left(u)):
            copy.wait_send()
        return 0

    lax.fori_loop(0, 8, settle, 0)
    for q in range(2):
        for k in range(1, 8):
            vision_part(q, k).wait_send()
            back_part(q, k).wait_send()
    xhat, rstd = normalize(attn_ref[...].reshape(VISION_WIDTH, 256), eye(256))
    take = mm_nt(eye(512), granule_of_patch(slot_ref)).astype(BF16)
    for q in range(2):
        for kk in range(1 - q, 16):
            route_back(q, kk).wait()
    grads = mm(take, arrived[...].reshape(512, HALF))
    gy = jnp.concatenate([grads[:256], grads[256:]], axis=1) * mgain_ref[...]
    mean = jnp.mean(gy, axis=1, keepdims=True)
    along = jnp.mean(gy * xhat, axis=1, keepdims=True)
    out_ref[...] = (rstd * (gy - mean - xhat * along)).astype(BF16)


def params(collective_id=None):
    if collective_id is None:
        return pltpu.CompilerParams(vmem_limit_bytes=48 * 2**20)
    return pltpu.CompilerParams(
        vmem_limit_bytes=58 * 2**20, collective_id=collective_id, has_side_effects=True
    )


def shaped(*shape, dtype=BF16):
    return jax.ShapeDtypeStruct(shape, dtype)


def buffer(*shape):
    return pltpu.VMEM(shape, BF16)


def body(
    queries,
    key_rows,
    values,
    segment_ids,
    merger_norm_gain,
    merge_weight,
    text_rows,
    token_gain,
    cotangent,
    send_slot,
    place_pos,
):
    w = lax.all_gather(merge_weight, "grp", axis=0, tiled=True)
    gain = merger_norm_gain.reshape(1, VISION_WIDTH)
    slot = send_slot.reshape(1, ROWS)

    x = pl.pallas_call(
        heads_out,
        out_shape=shaped(8, 496, 256),
        in_specs=[VMEM] * 4,
        out_specs=VMEM,
        scratch_shapes=[buffer(8, 496, 256), DMA((8,)), DMA((8,)), DMA(())],
        compiler_params=params(1),
        name="heads_out",
    )(queries, key_rows, values, segment_ids.reshape(1, 256))
    o = pl.pallas_call(
        attention,
        out_shape=shaped(8, 160, 256),
        in_specs=[VMEM],
        out_specs=VMEM,
        scratch_shapes=[
            pltpu.VMEM((8, 2, 256, HEAD_DIM), BF16),
            pltpu.VMEM((8, 256, 128), F32),
            pltpu.VMEM((2, 8, 256, 256), F32),
        ],
        compiler_params=params(),
        name="attention",
    )(x)
    attn, a = pl.pallas_call(
        merge_and_gather,
        out_shape=[shaped(8, 160, 256), shaped(2, 8, PART, MERGER_FEATURES)],
        in_specs=[VMEM] * 3,
        out_specs=[VMEM] * 2,
        scratch_shapes=[
            buffer(32, 16, HALF),
            buffer(2, 16, 16, HALF),
            DMA((8,)),
            DMA((8,)),
            DMA((2, 16)),
            DMA((2, 16)),
            DMA(()),
            DMA((9, 2, 2)),
            DMA((9, 2, 2)),
        ],
        compiler_params=params(2),
        name="merge_and_gather",
    )(o, gain, slot)
    return pl.pallas_call(
        language,
        out_shape=[shaped(128, 8192), shaped(256, VISION_WIDTH)],
        in_specs=[VMEM] + [ANY] * 3 + [VMEM] * 5,
        out_specs=[VMEM] * 2,
        scratch_shapes=[
            buffer(MERGER_FEATURES, 1024),
            buffer(128, 8192),
            buffer(128, 8192),
            buffer(8, ROWS, 1024),
            buffer(2, 8, PART, 1024),
            buffer(2, 8, PART, 1024),
            buffer(2, 8, PART, 1024),
            buffer(2, 8, PART, 1024),
            buffer(8, 2, 4, 2, PART, HALF),
            buffer(8, 4, 2, PART, HALF),
            buffer(8, 2, PART, HALF),
            buffer(8, 2, 2, PART, HALF),
            buffer(2, 4, 2, PART, HALF),
            buffer(2, 16, 16, HALF),
            buffer(32, 16, HALF),
            DMA((2,)),
            DMA((2,)),
            DMA((2, 8)),
            DMA((2, 8)),
            DMA((2, 8)),
            DMA((2, 8)),
            DMA((5, 8)),
            DMA((5, 8)),
            DMA((2, 16)),
            DMA((2, 16)),
            DMA(()),
        ],
        compiler_params=params(3),
        name="language",
    )(
        a,
        w,
        text_rows,
        cotangent,
        token_gain.reshape(1, 8192),
        place_pos.reshape(1, ROWS),
        attn,
        gain,
        slot,
    )


def solution(mesh):
    in_specs = (
        P(("grp", "seq"), None),
        P(("grp", "seq"), None),
        P(("grp", "seq"), None),
        P(("grp", "seq")),
        P(),
        P("grp", "seq"),
        P(("grp", "seq"), None),
        P(),
        P(("grp", "seq"), None),
        P(("grp", "seq")),
        P(("grp", "seq")),
    )
    out_specs = (P(("grp", "seq"), None), P(("grp", "seq"), None))
    return jax.shard_map(body, mesh=mesh, in_specs=in_specs, out_specs=out_specs, check_vma=False)
```

time: 243 us -> 224 us (0.922)
  Pallas kernels: 216 us -> 197 us
  waiting for transfers between devices: 0.68 us -> 4.06 us
    pallas_call x1, Pallas kernels: 89.2 us -> 75.5 us  [body(): pl.pallas_call(language, out_shape=[shaped(128, 8192), shaped(256, VISION...]
    pallas_call x1, Pallas kernels: 17.2 us -> 11.9 us  [body(): pl.pallas_call(attention, out_shape=shaped(8, 160, 256), in_specs=[VMEM],...]
    all_gather x1, waiting for transfers between devices: 0.01 us -> 3.38 us  [body(): w = lax.all_gather(merge_weight, 'grp', axis=0, tiled=True)]
    unnamed x11 -> x8, local copies, waits for them, and re-layouts: 6.57 us -> 6.43 us
  transfers between devices with their start and end apart: 1 -> 1, of which waited for: 0 -> 1; matrix products, arithmetic and copies ran while one was open for 2% -> 1% of each run, Pallas kernels for 52% -> 55%
where the time goes in v3:
time: 224 us; the launch traced here: 223 us
  Pallas kernels  197 us (88%)
  between operations  14.1 us (6%)
  local copies, waits for them, and re-layouts  7.73 us (3%)
  waiting for transfers between devices  4.06 us (2%)
    pallas_call x1, Pallas kernels, body(): pl.pallas_call(merge_and_gather, out_shape=[shaped(8, 160, 256), shaped(2...  81.5 us
    pallas_call x1, Pallas kernels, body(): pl.pallas_call(language, out_shape=[shaped(128, 8192), shaped(256, VISION...  75.5 us
    pallas_call x1, Pallas kernels, body(): pl.pallas_call(heads_out, out_shape=shaped(8, 496, 256), in_specs=[VMEM]...  28.3 us
    pallas_call x1, Pallas kernels, body(): pl.pallas_call(attention, out_shape=shaped(8, 160, 256), in_specs=[VMEM],...  11.9 us
    unnamed x8, local copies, waits for them, and re-layouts  6.43 us
  transfers between devices with their start and end apart: 1, of which 1 were waited for; matrix products, arithmetic and copies ran while one was open for 1% of the time, Pallas kernels for 55%

profile of v3, /device:TPU:2, one launch (start us, length us, event | category | flops | bytes accessed | tf_op | source)
XLA Modules:
  0.0 223.1 jit_solution(1859875227649545340)
XLA Ops:
  7.2 0.0 all-gather.2.cloned.1.call-start
  7.2 0.7 all-gather.2.cloned.1.call-update
  7.9 1.3 reshape.20.gain_ref.mgain_ref
  9.2 28.3 %heads_out.1.x_ref = bf16[8,496,256]{2,1,0:T(8,128)(2,1)} custom-call(bf16[256,1280]{1,0:T(8,128)(2,1)} %q_ref.1, bf16[256,1280]{1,0:T(8,128)(2,1)} %k_ref.1, bf16[256,1280]{1,0:T(8,128)(2,1)} %v_ref.1, s32[1,256]{1,0:T(1,128)} %bitcast.7), custom_call_target="tpu_custom_call" | custom-call | tf_op jit(solution)/shard_map/heads_out/pallas_call | solution.py:519
  37.5 0.0 copy-start
  37.5 1.6 copy-done
  39.1 11.9 %attention.1.o_ref = bf16[8,160,256]{2,1,0:T(8,128)(2,1)S(1)} custom-call(bf16[8,496,256]{2,1,0:T(8,128)(2,1)S(1)} %copy-done), custom_call_target="tpu_custom_call" | custom-call | tf_op jit(solution)/shard_map/attention/pallas_call | solution.py:528
  51.0 0.0 copy-start.1
  51.0 0.8 copy-done.1
  51.9 81.5 %merge_and_gather.1 = (bf16[8,160,256]{2,1,0:T(8,128)(2,1)}, bf16[2,8,32,5120]{3,2,1,0:T(8,128)(2,1)}) custom-call(bf16[8,160,256]{2,1,0:T(8,128)(2,1)} %copy-done.1, f32[1,1280]{1,0:T(1,128)} %reshape.20.gain_ref.mgain_ref, s32[1,64]{1,0:T(1,128)} %bitcast.5), custom_call_target="tpu_custom_call" | custom-call | tf_op jit(solution)/shard_map/merge_and_gather/pallas_call | solution.py:541
  133.4 3.4 %all-gather.2.cloned.1.call-done.w_ref = bf16[5120,1024]{1,0:T(8,128)(2,1)} async-done(((bf16[160,1024]{1,0:T(8,128)(2,1)}), bf16[5120,1024]{1,0:T(8,128)(2,1)}) %all-gather.2.cloned.1.call-update) | async-done | bytes 10485776 | tf_op jit(solution)/shard_map/all_gather | solution.py:515
  136.8 75.5 %language.1 = (bf16[128,8192]{1,0:T(8,128)(2,1)}, bf16[256,1280]{1,0:T(8,128)(2,1)}) custom-call(bf16[2,8,32,5120]{3,2,1,0:T(8,128)(2,1)} %get-tuple-element.4.a_ref, bf16[5120,1024]{1,0:T(8,128)(2,1)} %all-gather.2.cloned.1.call-done.w_ref, bf16[128,8192]{1,0:T(8,128)(2,1)} %text_ref.1, bf16[128,8192]{1,0:T(8,128)(2,1)} %cot_ref.1, f32[1,8192]{1,0:T(1,128)} %bitcast.4, ...), custom_call_target="tpu_custom_call" | custom-call | tf_op jit(solution)/shard_map/language/pallas_call | solution.py:560
  212.3 0.0 copy-start.2
  212.3 3.2 %copy.15 = bf16[128,8192]{1,0:T(8,128)(2,1)} copy(bf16[128,8192]{1,0:T(8,128)(2,1)} %get-tuple-element.8) | data formatting | bytes 4194304
  215.4 0.0 copy-done.2
  215.4 0.8 copy.16
Async XLA Ops:
  7.2 129.6 %all-gather.2.cloned.1.call-start = ((), (), s32[]{:S(2)}) async-start(), calls=%async_computation | async-start | bytes 10813440 | tf_op jit(solution)/shard_map/all_gather | solution.py:515
  37.5 1.6 copy-start
  51.0 0.8 copy-start.1
  212.3 3.2 %copy-start.2 = (bf16[256,1280]{1,0:T(8,128)(2,1)S(1)}, bf16[256,1280]{1,0:T(8,128)(2,1)}, u32[]{:S(2)}) copy-start(bf16[256,1280]{1,0:T(8,128)(2,1)} %get-tuple-element.9) | copy-start | bytes 1966084
Sparse Core Ops, SparseCore 0:
  10.6 126.1 all-gather.1

commit v4 on v3

--- a/solution.py
+++ b/solution.py
@@ -128,6 +128,11 @@
     return [{axis: lax.rem(me + k, n)} for k in range(1, n)]
 
 
+def sub_block_of_granule(rho):
+    n, half, i, p = rho // 16, rho // 8 % 2, rho // 4 % 2, rho % 4
+    return (p * 2 + half) * 16 + n * 2 + i
+
+
 def exchange(src, dst, send_sem, recv_sem, local_sem):
     me = lax.axis_index("seq")
     copies = []
@@ -269,16 +274,21 @@
 def language(
     a_ref, w_ref, text_ref, cot_ref, gain_ref, pos_ref, attn_ref, mgain_ref, slot_ref,
     hid_ref, out_ref,
-    w, text, cot, picked, proj, vis, back, ret, terms, twin_terms, far, near, summed, granules, arrived,
+    a, w, text, cot, picked, proj, vis, back, ret, terms, twin_terms, far, near, summed, granules, arrived,
     w_sem, t_sem, s1, r1, s2, r2, s3, r3, s4, r4, l_sem,
 ):
-    loads = [pltpu.make_async_copy(cot_ref, cot, t_sem.at[0])]
-    for n in range(2):
-        rows = pl.ds(2560 * n, 2560)
-        loads.append(pltpu.make_async_copy(w_ref.at[rows], w.at[rows], w_sem.at[n]))
-    loads.append(pltpu.make_async_copy(text_ref, text, t_sem.at[1]))
-    for load in loads:
-        load.start()
+    def load_w(n):
+        cols = pl.ds(pl.multiple_of(n * 256, 256), 256)
+        return pltpu.make_async_copy(w_ref.at[:, cols], w.at[:, cols], w_sem.at[n])
+
+    load_cot = pltpu.make_async_copy(cot_ref, cot, t_sem.at[0])
+    load_text = pltpu.make_async_copy(text_ref, text, t_sem.at[1])
+    load_a = pltpu.make_async_copy(a_ref, a, t_sem.at[2])
+    load_a.start()
+    for n in range(4):
+        load_w(n).start()
+    load_cot.start()
+    load_text.start()
     greet(others("seq", 8) + others("grp", 32))
     me, right, left, across, twin = neighbours()
     g = lax.axis_index("grp")
@@ -289,64 +299,38 @@
     place = mm(place, onehot(iota((ROWS, ROWS), 0) == turned)).astype(BF16)
     pick = mm_nt(eye(ROWS), place).astype(BF16)
     taken = jnp.sum(place.astype(F32), axis=1, keepdims=True) > 0.5
-    loads[0].wait()
+    load_a.wait()
+
+    def vision_tile(n, k):
+        d = lax.rem(me + k, 8)
+        return remote(proj.at[n, d], vis.at[n, me], s1.at[n, k], r1.at[n, k], {"seq": d})
+
+    def project(n, _):
+        load_w(n).wait()
+        cols = pl.ds(pl.multiple_of(n * 256, 256), 256)
+        total = mm(a[...].reshape(512, MERGER_FEATURES), w[:, cols]).astype(BF16)
+        for q in range(2):
+            for d in range(8):
+                row = PART * (8 * q + d)
+                proj[n, d, q] = total[row : row + PART]
+        for k in range(1, 8):
+            vision_tile(n, k).start()
+        vis[n, me] = proj[n, me]
+        return 0
+
+    lax.fori_loop(0, 4, project, 0)
+    load_cot.wait()
     for c in range(8):
-        picked[c] = mm(pick, cot[:, 1024 * c : 1024 * c + 1024]).astype(BF16)
-    for load in loads[1:]:
-        load.wait()
-
-    def vision_part(q, k):
-        d = lax.rem(me + k, 8)
-        return remote(proj.at[q, d], vis.at[q, me], s1.at[q, k], r1.at[q, k], {"seq": d})
-
-    def project(q, _):
-        rows = a_ref[q].reshape(256, MERGER_FEATURES)
         for n in range(4):
-            cols = slice(256 * n, 256 * n + 256)
-            proj[q, :, :, cols] = mm(rows, w[:, cols]).astype(BF16).reshape(8, PART, 256)
-        for k in range(1, 8):
-            vision_part(q, k).start()
-        vis[q, me] = proj[q, me]
-        return 0
-
-    lax.fori_loop(0, 2, project, 0)
+            picked[n, c] = mm(pick, cot[:, 1024 * c + 256 * n : 1024 * c + 256 * n + 256]).astype(BF16)
+    load_text.wait()
 
     def back_part(q, k):
         d = lax.rem(me + k, 8)
         return remote(back.at[q, d], ret.at[q, me], s2.at[q, k], r2.at[q, k], {"seq": d})
 
-    def gains(c):
-        return gain_ref[:, pl.ds(pl.multiple_of(c * 1024, 1024), 1024)]
-
-    scales = []
-    for q in range(2):
-        rows = slice(PART * q, PART * q + PART)
-        for k in range(1, 8):
-            vision_part(q, k).wait_recv()
-
-        def sums(c, carry):
-            v = vis[q, c].astype(F32)
-            gy = picked[c, rows].astype(F32) * gains(c)
-            return carry[0] + v * v, carry[1] + gy * v
-
-        zero = jnp.zeros((PART, 1024), F32)
-        squares, products = lax.fori_loop(0, 8, sums, (zero, zero))
-        r = lax.rsqrt(jnp.sum(squares, axis=1, keepdims=True) / 8192.0 + EPS)
-        slope = r * r * (jnp.sum(products, axis=1, keepdims=True) / 8192.0)
-        scales.append(r)
-
-        def grads(c):
-            gy = picked[c, rows].astype(F32) * gains(c)
-            return (r * (gy - vis[q, c].astype(F32) * slope)).astype(BF16)
-
-        def send(k, _):
-            d = lax.rem(me + k, 8)
-            back[q, d] = grads(d)
-            back_part(q, k).start()
-            return 0
-
-        lax.fori_loop(1, 8, send, 0)
-        ret[q, me] = grads(me)
+    def gains(c, n):
+        return gain_ref[:, pl.ds(pl.multiple_of(c * 1024 + n * 256, 256), 256)]
 
     def text_squares(c, carry):
         t = text[:, pl.ds(pl.multiple_of(c * 1024, 1024), 1024)].astype(F32)
@@ -354,35 +338,64 @@
 
     r_text = lax.rsqrt(lax.fori_loop(0, 8, text_squares, jnp.zeros((128, 1), F32)) / 8192.0 + EPS)
 
-    def hidden(c, _):
-        cols = pl.ds(pl.multiple_of(c * 1024, 1024), 1024)
-        gain = gains(c)
-        rows = jnp.concatenate([vis[q, c].astype(F32) * scales[q] for q in range(2)], axis=0) * gain
-        rows = mm(place, rows.astype(BF16))
-        hid_ref[:, cols] = jnp.where(taken, rows, text[:, cols].astype(F32) * r_text * gain).astype(BF16)
-        return 0
-
-    lax.fori_loop(0, 8, hidden, 0)
+    def tile_sums(n, carry):
+        for k in range(1, 8):
+            vision_tile(n, k).wait_recv()
+
+        def sums(c, carry):
+            v = vis[n, c].reshape(ROWS, 256).astype(F32)
+            gy = picked[n, c].astype(F32) * gains(c, n)
+            return carry[0] + v * v, carry[1] + gy * v
+
+        return lax.fori_loop(0, 8, sums, carry)
+
+    zero = jnp.zeros((ROWS, 256), F32)
+    squares, products = lax.fori_loop(0, 4, tile_sums, (zero, zero))
+    r = lax.rsqrt(jnp.sum(squares, axis=1, keepdims=True) / 8192.0 + EPS)
+    slope = r * r * (jnp.sum(products, axis=1, keepdims=True) / 8192.0)
+
+    for q in range(2):
+        rows = slice(PART * q, PART * q + PART)
+
+        def grads(c, ref):
+            for n in range(4):
+                gy = picked[n, c, rows].astype(F32) * gains(c, n)
+                grad = r[rows] * (gy - vis[n, c, q].astype(F32) * slope[rows])
+                ref[:, 256 * n : 256 * n + 256] = grad.astype(BF16)
+
+        def send(k, _):
+            d = lax.rem(me + k, 8)
+            grads(d, back.at[q, d])
+            back_part(q, k).start()
+            return 0
+
+        lax.fori_loop(1, 8, send, 0)
+        grads(me, ret.at[q, me])
+
+    def hidden(c):
+        for n in range(4):
+            cols = pl.ds(pl.multiple_of(c * 1024 + n * 256, 256), 256)
+            gain = gains(c, n)
+            rows = (vis[n, c].reshape(ROWS, 256).astype(F32) * r * gain).astype(BF16)
+            own = (text[:, cols].astype(F32) * r_text * gain).astype(BF16)
+            hid_ref[:, cols] = jnp.where(taken, mm(place, rows), own.astype(F32)).astype(BF16)
 
     core = lax.rem(me, 2)
     x = me // 2
     chip_right, chip_left, chip_across = lax.rem(x + 1, 4), lax.rem(x + 3, 4), lax.rem(x + 2, 4)
-    upper, lower = pl.ds(0, 16), pl.ds(16, 16)
-    halves = pl.ds(0, 2)
+    upper, lower = pl.ds(0, 2), pl.ds(2, 2)
 
     def to_twin(u):
         return remote(terms.at[u, 1 - core], twin_terms.at[u], s3.at[0, u], r3.at[0, u], {"seq": twin})
 
     def far_right(u):
         return remote(
-            terms.at[u, core, chip_across, halves, upper], far.at[u, halves, upper],
-            s3.at[1, u], r3.at[1, u], {"seq": right},
+            terms.at[u, core, chip_across, upper], far.at[u, upper], s3.at[1, u], r3.at[1, u], {"seq": right}
         )
 
     def far_left(u):
         return remote(
-            terms.at[u, core, chip_across, halves, lower], far.at[u, halves, lower],
-            s3.at[2, u], r3.at[2, u], {"seq": left},
+            terms.at[u, core, chip_across, lower], far.at[u, lower], s3.at[2, u], r3.at[2, u], {"seq": left}
         )
 
     def near_right(u):
@@ -391,19 +404,19 @@
     def near_left(u):
         return remote(terms.at[u, core, chip_left], near.at[u, 1], s3.at[4, u], r3.at[4, u], {"seq": left})
 
-    to_granule = onehot(block_of_granule(iota((256, 256), 0)) == iota((256, 256), 1))
-
-    def route_back(q, kk):
-        d = lax.rem(g + 32 - (2 * kk + q), 32)
-        return remote(granules.at[q, kk], arrived.at[g], s4.at[q, kk], r4.at[q, kk], {"grp": d})
-
-    def send_back(q):
-        rows = mm(to_granule, summed[q].reshape(256, HALF)).astype(BF16)
-        granules[q] = rows.reshape(16, 16, HALF)
-        if q == 0:
+    to_granule = onehot(sub_block_of_granule(iota((128, 128), 0)) == iota((128, 128), 1))
+
+    def route_back(t, n):
+        d = lax.rem(g + 32 - (2 * (t % 2 * 8 + n) + t // 2), 32)
+        return remote(granules.at[t, n], arrived.at[g], s4.at[t, n], r4.at[t, n], {"grp": d})
+
+    def send_back(t):
+        rows = mm(to_granule, summed[t].reshape(128, HALF)).astype(BF16)
+        granules[t] = rows.reshape(8, 16, HALF)
+        if t == 0:
             arrived[g] = granules[0, 0]
-        for kk in range(1 - q, 16):
-            route_back(q, kk).start()
+        for n in range(1 if t == 0 else 0, 8):
+            route_back(t, n).start()
 
     def step(i, _):
         for q in range(2):
@@ -415,12 +428,14 @@
         @pl.when(i < 8)
         def _():
             u = i
-            rows = pl.ds(pl.multiple_of(lax.rem(u, 4) * 1280, 1280), 1280)
-            total = mm_nt(ret[u // 4].reshape(256, 1024), w[rows, :]).astype(BF16)
+            rows = pl.ds(pl.multiple_of(lax.rem(u, 2) * 2560, 2560), 2560)
+            own = pl.ds(pl.multiple_of(lax.rem(u // 2, 2) * 16, 16), 16)
+            total = mm_nt(ret[u // 4, :, own, :].reshape(128, 1024), w[rows, :]).astype(BF16)
             for s in range(8):
-                for b in range(2):
-                    terms[u, s % 2, s // 2, b] = total[PART * s : PART * s + PART, HALF * b : HALF * b + HALF]
+                for b in range(4):
+                    terms[u, s % 2, s // 2, b] = total[16 * s : 16 * s + 16, HALF * b : HALF * b + HALF]
             to_twin(u).start()
+            hidden(u)
 
         @pl.when((i >= 1) & (i < 9))
         def _():
@@ -434,13 +449,13 @@
         def _():
             u = i - 2
             far_right(u).wait_recv()
-            terms[u, core, chip_right, :, upper] = (
-                terms[u, core, chip_right, :, upper].astype(F32) + far[u, :, upper].astype(F32)
+            terms[u, core, chip_right, upper] = (
+                terms[u, core, chip_right, upper].astype(F32) + far[u, upper].astype(F32)
             ).astype(BF16)
             near_right(u).start()
             far_left(u).wait_recv()
-            terms[u, core, chip_left, :, lower] = (
-                terms[u, core, chip_left, :, lower].astype(F32) + far[u, :, lower].astype(F32)
+            terms[u, core, chip_left, lower] = (
+                terms[u, core, chip_left, lower].astype(F32) + far[u, lower].astype(F32)
             ).astype(BF16)
             near_left(u).start()
 
@@ -450,16 +465,17 @@
             near_right(u).wait_recv()
             near_left(u).wait_recv()
             total = terms[u, core, x].astype(F32) + near[u, 0].astype(F32) + near[u, 1].astype(F32)
-            summed[u // 4, lax.rem(u, 4)] = total.astype(BF16)
-
-        @pl.when(i == 6)
-        def _():
-            send_back(0)
+            summed[u // 2, lax.rem(u, 2)] = total.astype(BF16)
+
+        for t in range(3):
+            @pl.when(i == 2 * t + 4)
+            def _():
+                send_back(t)
 
         return 0
 
     lax.fori_loop(0, 11, step, 0)
-    send_back(1)
+    send_back(3)
 
     def settle(u, _):
         for copy in (to_twin(u), far_right(u), far_left(u), near_right(u), near_left(u)):
@@ -469,13 +485,15 @@
     lax.fori_loop(0, 8, settle, 0)
     for q in range(2):
         for k in range(1, 8):
-            vision_part(q, k).wait_send()
             back_part(q, k).wait_send()
+    for n in range(4):
+        for k in range(1, 8):
+            vision_tile(n, k).wait_send()
     xhat, rstd = normalize(attn_ref[...].reshape(VISION_WIDTH, 256), eye(256))
     take = mm_nt(eye(512), granule_of_patch(slot_ref)).astype(BF16)
-    for q in range(2):
-        for kk in range(1 - q, 16):
-            route_back(q, kk).wait()
+    for t in range(4):
+        for n in range(1 if t == 0 else 0, 8):
+            route_back(t, n).wait()
     grads = mm(take, arrived[...].reshape(512, HALF))
     gy = jnp.concatenate([grads[:256], grads[256:]], axis=1) * mgain_ref[...]
     mean = jnp.mean(gy, axis=1, keepdims=True)
@@ -560,34 +578,35 @@
     return pl.pallas_call(
         language,
         out_shape=[shaped(128, 8192), shaped(256, VISION_WIDTH)],
-        in_specs=[VMEM] + [ANY] * 3 + [VMEM] * 5,
+        in_specs=[ANY] * 4 + [VMEM] * 5,
         out_specs=[VMEM] * 2,
         scratch_shapes=[
+            buffer(2, 8, PART, MERGER_FEATURES),
             buffer(MERGER_FEATURES, 1024),
             buffer(128, 8192),
             buffer(128, 8192),
-            buffer(8, ROWS, 1024),
+            buffer(4, 8, ROWS, 256),
+            buffer(4, 8, 2, PART, 256),
+            buffer(4, 8, 2, PART, 256),
             buffer(2, 8, PART, 1024),
             buffer(2, 8, PART, 1024),
-            buffer(2, 8, PART, 1024),
-            buffer(2, 8, PART, 1024),
-            buffer(8, 2, 4, 2, PART, HALF),
-            buffer(8, 4, 2, PART, HALF),
-            buffer(8, 2, PART, HALF),
-            buffer(8, 2, 2, PART, HALF),
-            buffer(2, 4, 2, PART, HALF),
-            buffer(2, 16, 16, HALF),
+            buffer(8, 2, 4, 4, 16, HALF),
+            buffer(8, 4, 4, 16, HALF),
+            buffer(8, 4, 16, HALF),
+            buffer(8, 2, 4, 16, HALF),
+            buffer(4, 2, 4, 16, HALF),
+            buffer(4, 8, 16, HALF),
             buffer(32, 16, HALF),
-            DMA((2,)),
-            DMA((2,)),
-            DMA((2, 8)),
-            DMA((2, 8)),
+            DMA((4,)),
+            DMA((3,)),
+            DMA((4, 8)),
+            DMA((4, 8)),
             DMA((2, 8)),
             DMA((2, 8)),
             DMA((5, 8)),
             DMA((5, 8)),
-            DMA((2, 16)),
-            DMA((2, 16)),
+            DMA((4, 8)),
+            DMA((4, 8)),
             DMA(()),
         ],
         compiler_params=params(3),

time: 224 us -> 219 us (0.978)
  Pallas kernels: 197 us -> 186 us
  waiting for transfers between devices: 4.06 us -> 11.4 us
    pallas_call x1, Pallas kernels: 81.5 us -> 65.3 us  [body(): pl.pallas_call(merge_and_gather, out_shape=[shaped(8, 160, 256), shaped(2...]
    all_gather x1, waiting for transfers between devices: 3.38 us -> 10.7 us  [body(): w = lax.all_gather(merge_weight, 'grp', axis=0, tiled=True)]
    pallas_call x1, Pallas kernels: 11.9 us -> 17.2 us  [body(): pl.pallas_call(attention, out_shape=shaped(8, 160, 256), in_specs=[VMEM],...]
  transfers between devices with their start and end apart: 1 -> 1, of which waited for: 1 -> 1; matrix products, arithmetic and copies ran while one was open for 1% -> 1% of each run, Pallas kernels for 55% -> 51%
where the time goes in v4:
time: 219 us
  Pallas kernels  186 us (85%)
  between operations  14.1 us (6%)
  waiting for transfers between devices  11.4 us (5%)
  local copies, waits for them, and re-layouts  7.73 us (4%)
    pallas_call x1, Pallas kernels, body(): pl.pallas_call(language, out_shape=[shaped(128, 8192), shaped(256, VISION...  74.9 us
    pallas_call x1, Pallas kernels, body(): pl.pallas_call(merge_and_gather, out_shape=[shaped(8, 160, 256), shaped(2...  65.3 us
    pallas_call x1, Pallas kernels, body(): pl.pallas_call(heads_out, out_shape=shaped(8, 496, 256), in_specs=[VMEM]...  28.3 us
    pallas_call x1, Pallas kernels, body(): pl.pallas_call(attention, out_shape=shaped(8, 160, 256), in_specs=[VMEM],...  17.2 us
    all_gather x1, waiting for transfers between devices, body(): w = lax.all_gather(merge_weight, 'grp', axis=0, tiled=True)  10.7 us
    unnamed x8, local copies, waits for them, and re-layouts  6.43 us
  transfers between devices with their start and end apart: 1, of which 1 were waited for; matrix products, arithmetic and copies ran while one was open for 1% of the time, Pallas kernels for 51%

profile of v4, /device:TPU:2, one launch (start us, length us, event | category | flops | bytes accessed | tf_op | source)
XLA Modules:
  0.0 218.9 jit_solution(2921886523965948298)
XLA Ops:
  7.2 0.0 all-gather.2.cloned.1.call-start
  7.2 0.7 all-gather.2.cloned.1.call-update
  7.9 1.3 reshape.20.gain_ref.mgain_ref
  9.2 28.3 %heads_out.1.x_ref = bf16[8,496,256]{2,1,0:T(8,128)(2,1)} custom-call(bf16[256,1280]{1,0:T(8,128)(2,1)} %q_ref.1, bf16[256,1280]{1,0:T(8,128)(2,1)} %k_ref.1, bf16[256,1280]{1,0:T(8,128)(2,1)} %v_ref.1, s32[1,256]{1,0:T(1,128)} %bitcast.7), custom_call_target="tpu_custom_call" | custom-call | tf_op jit(solution)/shard_map/heads_out/pallas_call | solution.py:537
  37.5 0.0 copy-start
  37.5 1.6 copy-done
  39.1 17.2 %attention.1.o_ref = bf16[8,160,256]{2,1,0:T(8,128)(2,1)S(1)} custom-call(bf16[8,496,256]{2,1,0:T(8,128)(2,1)S(1)} %copy-done), custom_call_target="tpu_custom_call" | custom-call | tf_op jit(solution)/shard_map/attention/pallas_call | solution.py:546
  56.3 0.0 copy-start.1
  56.3 0.8 copy-done.1
  57.1 65.3 %merge_and_gather.1 = (bf16[8,160,256]{2,1,0:T(8,128)(2,1)}, bf16[2,8,32,5120]{3,2,1,0:T(8,128)(2,1)}) custom-call(bf16[8,160,256]{2,1,0:T(8,128)(2,1)} %copy-done.1, f32[1,1280]{1,0:T(1,128)} %reshape.20.gain_ref.mgain_ref, s32[1,64]{1,0:T(1,128)} %bitcast.5), custom_call_target="tpu_custom_call" | custom-call | tf_op jit(solution)/shard_map/merge_and_gather/pallas_call | solution.py:559
  122.4 10.7 %all-gather.2.cloned.1.call-done.w_ref = bf16[5120,1024]{1,0:T(8,128)(2,1)} async-done(((bf16[160,1024]{1,0:T(8,128)(2,1)}), bf16[5120,1024]{1,0:T(8,128)(2,1)}) %all-gather.2.cloned.1.call-update) | async-done | bytes 10485776 | tf_op jit(solution)/shard_map/all_gather | solution.py:533
  133.1 74.9 %language.1 = (bf16[128,8192]{1,0:T(8,128)(2,1)}, bf16[256,1280]{1,0:T(8,128)(2,1)}) custom-call(bf16[2,8,32,5120]{3,2,1,0:T(8,128)(2,1)} %get-tuple-element.4.a_ref, bf16[5120,1024]{1,0:T(8,128)(2,1)} %all-gather.2.cloned.1.call-done.w_ref, bf16[128,8192]{1,0:T(8,128)(2,1)} %text_ref.1, bf16[128,8192]{1,0:T(8,128)(2,1)} %cot_ref.1, f32[1,8192]{1,0:T(1,128)} %bitcast.4, ...), custom_call_target="tpu_custom_call" | custom-call | tf_op jit(solution)/shard_map/language/pallas_call | solution.py:578
  208.1 0.0 copy-start.2
  208.1 3.2 %copy.15 = bf16[128,8192]{1,0:T(8,128)(2,1)} copy(bf16[128,8192]{1,0:T(8,128)(2,1)} %get-tuple-element.8) | data formatting | bytes 4194304
  211.2 0.0 copy-done.2
  211.3 0.8 copy.16
Async XLA Ops:
  7.2 126.0 %all-gather.2.cloned.1.call-start = ((), (), s32[]{:S(2)}) async-start(), calls=%async_computation | async-start | bytes 10813440 | tf_op jit(solution)/shard_map/all_gather | solution.py:533
  37.5 1.6 copy-start
  56.3 0.8 copy-start.1
  208.1 3.2 %copy-start.2 = (bf16[256,1280]{1,0:T(8,128)(2,1)S(1)}, bf16[256,1280]{1,0:T(8,128)(2,1)}, u32[]{:S(2)}) copy-start(bf16[256,1280]{1,0:T(8,128)(2,1)} %get-tuple-element.9) | copy-start | bytes 1966084
Sparse Core Ops, SparseCore 0:
  10.6 122.5 all-gather.1

commit v5 on v4

--- a/solution.py
+++ b/solution.py
@@ -275,7 +275,7 @@
     a_ref, w_ref, text_ref, cot_ref, gain_ref, pos_ref, attn_ref, mgain_ref, slot_ref,
     hid_ref, out_ref,
     a, w, text, cot, picked, proj, vis, back, ret, terms, twin_terms, far, near, summed, granules, arrived,
-    w_sem, t_sem, s1, r1, s2, r2, s3, r3, s4, r4, l_sem,
+    w_sem, t_sem, s1, r1, s2, r2, s3, r3, s4, r4, h_sem, attn,
 ):
     def load_w(n):
         cols = pl.ds(pl.multiple_of(n * 256, 256), 256)
@@ -289,6 +289,8 @@
         load_w(n).start()
     load_cot.start()
     load_text.start()
+    load_attn = pltpu.make_async_copy(attn_ref, attn, t_sem.at[3])
+    load_attn.start()
     greet(others("seq", 8) + others("grp", 32))
     me, right, left, across, twin = neighbours()
     g = lax.axis_index("grp")
@@ -372,13 +374,18 @@
         lax.fori_loop(1, 8, send, 0)
         grads(me, ret.at[q, me])
 
+    def hidden_out(c):
+        cols = pl.ds(pl.multiple_of(c * 1024, 1024), 1024)
+        return pltpu.make_async_copy(text.at[:, cols], hid_ref.at[:, cols], h_sem.at[c])
+
     def hidden(c):
         for n in range(4):
             cols = pl.ds(pl.multiple_of(c * 1024 + n * 256, 256), 256)
             gain = gains(c, n)
             rows = (vis[n, c].reshape(ROWS, 256).astype(F32) * r * gain).astype(BF16)
             own = (text[:, cols].astype(F32) * r_text * gain).astype(BF16)
-            hid_ref[:, cols] = jnp.where(taken, mm(place, rows), own.astype(F32)).astype(BF16)
+            text[:, cols] = jnp.where(taken, mm(place, rows), own.astype(F32)).astype(BF16)
+        hidden_out(c).start()
 
     core = lax.rem(me, 2)
     x = me // 2
@@ -480,6 +487,7 @@
     def settle(u, _):
         for copy in (to_twin(u), far_right(u), far_left(u), near_right(u), near_left(u)):
             copy.wait_send()
+        hidden_out(u).wait()
         return 0
 
     lax.fori_loop(0, 8, settle, 0)
@@ -489,7 +497,8 @@
     for n in range(4):
         for k in range(1, 8):
             vision_tile(n, k).wait_send()
-    xhat, rstd = normalize(attn_ref[...].reshape(VISION_WIDTH, 256), eye(256))
+    load_attn.wait()
+    xhat, rstd = normalize(attn[...].reshape(VISION_WIDTH, 256), eye(256))
     take = mm_nt(eye(512), granule_of_patch(slot_ref)).astype(BF16)
     for t in range(4):
         for n in range(1 if t == 0 else 0, 8):
@@ -578,8 +587,8 @@
     return pl.pallas_call(
         language,
         out_shape=[shaped(128, 8192), shaped(256, VISION_WIDTH)],
-        in_specs=[ANY] * 4 + [VMEM] * 5,
-        out_specs=[VMEM] * 2,
+        in_specs=[ANY] * 4 + [VMEM] * 2 + [ANY] + [VMEM] * 2,
+        out_specs=[ANY, VMEM],
         scratch_shapes=[
             buffer(2, 8, PART, MERGER_FEATURES),
             buffer(MERGER_FEATURES, 1024),
@@ -598,7 +607,7 @@
             buffer(4, 8, 16, HALF),
             buffer(32, 16, HALF),
             DMA((4,)),
-            DMA((3,)),
+            DMA((4,)),
             DMA((4, 8)),
             DMA((4, 8)),
             DMA((2, 8)),
@@ -607,7 +616,8 @@
             DMA((5, 8)),
             DMA((4, 8)),
             DMA((4, 8)),
-            DMA(()),
+            DMA((8,)),
+            buffer(8, 160, 256),
         ],
         compiler_params=params(3),
         name="language",

time: 219 us -> 219 us (level)
    pallas_call x1, Pallas kernels: 65.3 us -> 71.6 us  [body(): pl.pallas_call(merge_and_gather, out_shape=[shaped(8, 160, 256), shaped(2...]
    pallas_call x1, Pallas kernels: 17.2 us -> 11 us  [body(): pl.pallas_call(attention, out_shape=shaped(8, 160, 256), in_specs=[VMEM],...]
where the time goes in v5:
time: 219 us
  Pallas kernels  186 us (85%)
  between operations  14.1 us (6%)
  waiting for transfers between devices  11.4 us (5%)
  local copies, waits for them, and re-layouts  7.73 us (4%)
    pallas_call x1, Pallas kernels, body(): pl.pallas_call(language, out_shape=[shaped(128, 8192), shaped(256, VISION...  74.6 us
    pallas_call x1, Pallas kernels, body(): pl.pallas_call(merge_and_gather, out_shape=[shaped(8, 160, 256), shaped(2...  71.6 us
    pallas_call x1, Pallas kernels, body(): pl.pallas_call(heads_out, out_shape=shaped(8, 496, 256), in_specs=[VMEM]...  28.3 us
    pallas_call x1, Pallas kernels, body(): pl.pallas_call(attention, out_shape=shaped(8, 160, 256), in_specs=[VMEM],...  11 us
    all_gather x1, waiting for transfers between devices, body(): w = lax.all_gather(merge_weight, 'grp', axis=0, tiled=True)  10.8 us
    unnamed x8, local copies, waits for them, and re-layouts  6.43 us
  transfers between devices with their start and end apart: 1, of which 1 were waited for; matrix products, arithmetic and copies ran while one was open for 1% of the time, Pallas kernels for 51%

profile of v5, /device:TPU:2, one launch (start us, length us, event | category | flops | bytes accessed | tf_op | source)
XLA Modules:
  0.0 218.8 jit_solution(9876019129536912469)
XLA Ops:
  7.2 0.0 all-gather.2.cloned.1.call-start
  7.2 0.7 all-gather.2.cloned.1.call-update
  7.9 1.3 reshape.20.gain_ref.mgain_ref
  9.2 28.3 %heads_out.1.x_ref = bf16[8,496,256]{2,1,0:T(8,128)(2,1)} custom-call(bf16[256,1280]{1,0:T(8,128)(2,1)} %q_ref.1, bf16[256,1280]{1,0:T(8,128)(2,1)} %k_ref.1, bf16[256,1280]{1,0:T(8,128)(2,1)} %v_ref.1, s32[1,256]{1,0:T(1,128)} %bitcast.7), custom_call_target="tpu_custom_call" | custom-call | tf_op jit(solution)/shard_map/heads_out/pallas_call | solution.py:546
  37.5 0.0 copy-start
  37.5 1.6 copy-done
  39.1 11.0 %attention.1.o_ref = bf16[8,160,256]{2,1,0:T(8,128)(2,1)S(1)} custom-call(bf16[8,496,256]{2,1,0:T(8,128)(2,1)S(1)} %copy-done), custom_call_target="tpu_custom_call" | custom-call | tf_op jit(solution)/shard_map/attention/pallas_call | solution.py:555
  50.1 0.0 copy-start.1
  50.2 0.8 copy-done.1
  51.0 71.6 %merge_and_gather.1 = (bf16[8,160,256]{2,1,0:T(8,128)(2,1)}, bf16[2,8,32,5120]{3,2,1,0:T(8,128)(2,1)}) custom-call(bf16[8,160,256]{2,1,0:T(8,128)(2,1)} %copy-done.1, f32[1,1280]{1,0:T(1,128)} %reshape.20.gain_ref.mgain_ref, s32[1,64]{1,0:T(1,128)} %bitcast.5), custom_call_target="tpu_custom_call" | custom-call | tf_op jit(solution)/shard_map/merge_and_gather/pallas_call | solution.py:568
  122.6 10.8 %all-gather.2.cloned.1.call-done.w_ref = bf16[5120,1024]{1,0:T(8,128)(2,1)} async-done(((bf16[160,1024]{1,0:T(8,128)(2,1)}), bf16[5120,1024]{1,0:T(8,128)(2,1)}) %all-gather.2.cloned.1.call-update) | async-done | bytes 10485776 | tf_op jit(solution)/shard_map/all_gather | solution.py:542
  133.3 74.6 %language.1 = (bf16[128,8192]{1,0:T(8,128)(2,1)}, bf16[256,1280]{1,0:T(8,128)(2,1)}) custom-call(bf16[2,8,32,5120]{3,2,1,0:T(8,128)(2,1)} %get-tuple-element.4.a_ref, bf16[5120,1024]{1,0:T(8,128)(2,1)} %all-gather.2.cloned.1.call-done.w_ref, bf16[128,8192]{1,0:T(8,128)(2,1)} %text_ref.1, bf16[128,8192]{1,0:T(8,128)(2,1)} %cot_ref.1, f32[1,8192]{1,0:T(1,128)} %bitcast.4, ...), custom_call_target="tpu_custom_call" | custom-call | tf_op jit(solution)/shard_map/language/pallas_call | solution.py:587
  208.0 0.0 copy-start.2
  208.0 3.2 %copy.15 = bf16[128,8192]{1,0:T(8,128)(2,1)} copy(bf16[128,8192]{1,0:T(8,128)(2,1)} %get-tuple-element.8) | data formatting | bytes 4194304
  211.1 0.0 copy-done.2
  211.1 0.8 copy.16
Async XLA Ops:
  7.2 126.2 %all-gather.2.cloned.1.call-start = ((), (), s32[]{:S(2)}) async-start(), calls=%async_computation | async-start | bytes 10813440 | tf_op jit(solution)/shard_map/all_gather | solution.py:542
  37.5 1.6 copy-start
  50.1 0.8 copy-start.1
  208.0 3.2 %copy-start.2 = (bf16[256,1280]{1,0:T(8,128)(2,1)S(1)}, bf16[256,1280]{1,0:T(8,128)(2,1)}, u32[]{:S(2)}) copy-start(bf16[256,1280]{1,0:T(8,128)(2,1)} %get-tuple-element.9) | copy-start | bytes 1966084
Sparse Core Ops, SparseCore 0:
  10.6 122.6 all-gather.1
